TPU v7x, 256 devices: a whole 4x4x8 slice. The times are simulated.
256 devices in a mesh: wide: 32 (over y_lo, z, core), blk: 8 (over y_hi, x).
Axes of the slice: x: 4, y: 4 (y_hi: 2, y_lo: 2; y = y_hi * 2 + y_lo), z: 8, core: 2. Of those that a mesh axis runs over, the one named last changes fastest.
Arguments:
- records: bfloat16 [8, 2304, 4, 8192], P('blk', 'wide'), may hold values from -6 to 6
- lengths: int32 [8, 2304], P('blk', 'wide'), may hold values from 8192 to 32768
- owners: int32 [8, 2304], P('blk', 'wide'), may hold values from -1 to 767, as said below
- own_pick: int32 [8, 32, 8, 2, 4], P('blk', 'wide'), may hold values from 0 to 23
- visit_pick: int32 [8, 32, 8, 2, 4], P('blk', 'wide'), may hold values from 0 to 23
- pair_mask: int32 [8, 32, 8, 2, 4, 4], P('blk', 'wide'), may hold values 0 or 1
Outputs:
- correlations: float32 [8, 32, 8, 2, 4, 4, 1024], P('blk', 'wide')
Inputs may be any that keep to these rules, and one draw needn't show every extreme that they name: `owners`: in each group every station number 0 to 767 is named by exactly one slot. A device's valid slots come first and its other slots hold -1. The busiest device of each group fills all 72 slots and two devices hold none. At most 3 slots of one device name stations of one owner (stations w * 24 to w * 24 + 23 belong to owner w), and this most is reached in every group.
All inputs are finite; a program needn't handle non-finite values. No bound on the sum of `pair_mask` on one device may be relied on, other than what follows from the above.
Results may differ from a plain program's by a relative error of at most 0.0049.
Values may be sent and summed in bfloat16 or wider, within the bound.
No kernel may reach another device: no remote copies, remote signals or barrier semaphores. Data moves between devices by JAX's collectives and lax.ppermute only.
A program may use at most 192 MiB of HBM per device.

v0:
```python
import functools
import math

import jax
import jax.numpy as jnp
import numpy as np
from jax import lax
from jax.experimental import pallas as pl
from jax.experimental.pallas import tpu as pltpu
from jax.sharding import PartitionSpec as P

ST_DEV = 24
SEG = 4
NT = 8192
NF = 4096
LAGS = 1024
ROWS = 64
LANES = 128
MOST = 6
SLOTS = (4, 3)
SPILL = 12
LAG_VMEM = 60 * 1024 * 1024
LEN_BITS = 16
NOTES = 16
SMEM = pl.BlockSpec(memory_space=pltpu.SMEM)
VMEM = pl.BlockSpec(memory_space=pltpu.VMEM)
ANY = pl.BlockSpec(memory_space=pl.ANY)


def split_bf16(values):
    high = values.astype(jnp.bfloat16)
    low = (values - high.astype(np.float64)).astype(jnp.bfloat16)
    return high, low


def transform_tables():
    first = np.arange(ROWS)
    second = np.arange(LANES)
    half = np.arange(LANES // 2)
    angle = 2.0 * math.pi / ROWS * (first[:, None] * first[None, :] % ROWS)
    wave = np.concatenate([np.cos(angle), -np.sin(angle)], 0)
    wave = np.einsum("ab,kn->aknb", np.eye(2), wave).reshape(4 * ROWS, 2 * ROWS)
    first_table = np.concatenate(split_bf16(wave), 1)
    twist = 2.0 * math.pi / NT * (first[:, None] * second[None, :] % NT)
    twist_table = np.stack([np.cos(twist), np.sin(twist)]).astype(np.float32)
    angle = 2.0 * math.pi / LANES * (second[:, None] * half[None, :] % LANES)
    cos, sin = np.cos(angle), np.sin(angle)
    wave = np.concatenate([np.concatenate([cos, -sin], 1), np.concatenate([sin, cos], 1)], 0)
    second_table = np.concatenate(split_bf16(wave), 1)
    return first_table, twist_table, second_table


def lag_tables():
    row = np.arange(ROWS // 2, dtype=np.int64)
    lane = np.arange(LANES, dtype=np.int64)
    bins = (row[:, None] + ROWS // 2 * (lane // ROWS)) + ROWS * (lane % ROWS)
    bins = bins.reshape(-1)
    weight = np.where(bins == 0, 0.5, 1.0).astype(np.float32) / np.float32(math.sqrt(NF * SEG))

    def at(delay):
        phase = bins[:, None] * delay[None, :] % NT
        return phase.astype(np.float32) * np.float32(2.0 * math.pi / NT)

    ahead = at(np.arange(LAGS // 2, dtype=np.int64))
    edge = at(np.array([NT - LAGS // 2], dtype=np.int64))
    cos = weight[:, None] * np.cos(ahead)
    sin = -weight[:, None] * np.sin(ahead)
    sin[:, :1] = -weight[:, None] * np.sin(edge)
    last = (weight[:, None] * np.cos(edge)).reshape(ROWS // 2, 1, LANES)
    return (
        np.concatenate([cos, sin], 0).astype(jnp.bfloat16),
        last.astype(jnp.bfloat16).astype(np.float32),
    )


def owner_of(value):
    return ((value >> LEN_BITS) * 2731) >> 16


def unit(slot):
    return pl.ds(pl.multiple_of(slot * ROWS, ROWS), ROWS)


def write_notes(out, begin, notes, flag, base):
    count = notes.shape[1]
    row = lax.broadcasted_iota(jnp.int32, (NOTES, LANES), 0)

    @pl.loop(0, notes.shape[0])
    def _(dev):
        tile = jnp.where(row == 3 * count, flag, base)
        for slot in range(count):
            value = notes[dev, slot]
            tile = jnp.where(row == 3 * slot, (value >> LEN_BITS) + 1, tile)
            tile = jnp.where(row == 3 * slot + 1, (value & 0xFFFF) >> 8, tile)
            tile = jnp.where(row == 3 * slot + 2, value & 0xFF, tile)
        out[dev, begin : begin + NOTES, :] = tile.astype(jnp.float32).astype(jnp.bfloat16)


def valid_slots(table, row):
    return table[row, table.shape[1] - 1]


def rows_kernel(low, count, table, core_ref, own, mate, out, fill, notes, started, sem):
    core = core_ref[0]
    started[0] = 0

    @pl.loop(0, out.shape[0])
    def _(dev):
        fill[dev] = 0
        for slot in range(count):
            notes[dev, slot] = -1

    def place(half, source):
        @pl.loop(0, valid_slots(table, half))
        def _(at):
            value = table[half, at]
            dev = owner_of(value)
            rank = fill[dev]
            fill[dev] = rank + 1

            @pl.when((rank >= low) & (rank < low + count))
            def _():
                started[0] += 1
                notes[dev, rank - low] = value - ((dev * ST_DEV) << LEN_BITS)
                rows = source.at[at, unit(core)]
                pltpu.make_async_copy(rows, out.at[dev, unit(rank - low)], sem).start()

    for half in range(2):

        @pl.when(core == half)
        def _():
            place(half, own)

        @pl.when(core != half)
        def _():
            place(half, mate)

    write_notes(out, count * ROWS, notes, 0, jnp.zeros((NOTES, LANES), jnp.int32))

    @pl.loop(0, started[0])
    def _(_):
        pltpu.make_async_copy(own.at[0, unit(0)], out.at[0, unit(0)], sem).wait()


def pack_rows(low, count, wide_count, table, core, own, mate):
    return pl.pallas_call(
        functools.partial(rows_kernel, low, count),
        out_shape=jax.ShapeDtypeStruct((wide_count, count * ROWS + NOTES, LANES), jnp.bfloat16),
        in_specs=[SMEM, SMEM, ANY, ANY],
        out_specs=VMEM,
        scratch_shapes=[
            pltpu.SMEM((wide_count,), jnp.int32),
            pltpu.SMEM((wide_count, count), jnp.int32),
            pltpu.SMEM((1,), jnp.int32),
            pltpu.SemaphoreType.DMA,
        ],
        cost_estimate=pl.CostEstimate(flops=0, bytes_accessed=wide_count * count * NT * 4, transcendentals=0),
        name="pack_rows",
    )(table, core, own, mate)


def plan_kernel(count, base_next, table, base, plan, tiles, fill, notes, theirs, flag):
    flag[0] = 0

    @pl.loop(0, fill.shape[0])
    def _(dev):
        fill[dev] = 0
        theirs[dev] = 0
        for slot in range(count):
            notes[dev, slot] = -1

    for half in range(2):

        @pl.loop(0, valid_slots(table, half))
        def _(at):
            value = table[half, at]
            dev = owner_of(value)
            rank = fill[dev]
            fill[dev] = rank + 1
            fits = rank < count
            plan[half, at] = jnp.where(fits, dev * 4 + rank, -1)

            @pl.when(fits)
            def _():
                notes[dev, rank] = value - ((dev * ST_DEV) << LEN_BITS)

            @pl.when(jnp.logical_not(fits))
            def _():
                flag[0] = 1

    for half in range(2):

        def check(at, index):
            dev = owner_of(table[2 + half, at])
            rank = theirs[dev]
            theirs[dev] = rank + 1
            spilled = rank >= base_next

            @pl.when(spilled & ((index >= SPILL) | (fill[dev] + rank >= 2 * base_next)))
            def _():
                flag[0] = 1

            return index + spilled.astype(jnp.int32)

        lax.fori_loop(0, valid_slots(table, 2 + half), check, 0)

    write_notes(tiles, 0, notes, flag[0], base[...])


def plan_rows(count, base_next, wide_count, table, base):
    return pl.pallas_call(
        functools.partial(plan_kernel, count, base_next),
        out_shape=(
            jax.ShapeDtypeStruct((2, table.shape[1] - 1), jnp.int32),
            jax.ShapeDtypeStruct((wide_count, NOTES, LANES), jnp.bfloat16),
            jax.ShapeDtypeStruct((wide_count,), jnp.int32),
        ),
        in_specs=[SMEM, VMEM],
        out_specs=(SMEM, VMEM, SMEM),
        scratch_shapes=[
            pltpu.SMEM((wide_count, count), jnp.int32),
            pltpu.SMEM((wide_count,), jnp.int32),
            pltpu.SMEM((1,), jnp.int32),
        ],
        cost_estimate=pl.CostEstimate(flops=2**16, bytes_accessed=2**18, transcendentals=0),
        name="plan_rows",
    )(table, base)


def first_kernel(count, table, plan, core_ref, own, mate, tiles, out, token, started, sem):
    core = core_ref[0]
    started[0] = 0
    token[0] = 0

    def place(half, source):
        @pl.loop(0, valid_slots(table, half))
        def _(at):
            code = plan[half, at]

            @pl.when(code >= 0)
            def _():
                started[0] += 1
                rows = source.at[at, unit(core)]
                pltpu.make_async_copy(rows, out.at[code >> 2, unit(code & 3)], sem).start()

    for half in range(2):

        @pl.when(core == half)
        def _():
            place(half, own)

        @pl.when(core != half)
        def _():
            place(half, mate)

    @pl.loop(0, out.shape[0], unroll=4)
    def _(dev):
        out[dev, count * ROWS :, :] = tiles[dev]

    @pl.loop(0, started[0])
    def _(_):
        pltpu.make_async_copy(own.at[0, unit(0)], out.at[0, unit(0)], sem).wait()


def pack_first(count, table, plan, core, own, mate, tiles):
    wide_count = tiles.shape[0]
    return pl.pallas_call(
        functools.partial(first_kernel, count),
        out_shape=(
            jax.ShapeDtypeStruct((wide_count, count * ROWS + NOTES, LANES), jnp.bfloat16),
            jax.ShapeDtypeStruct((1,), jnp.int32),
        ),
        in_specs=[SMEM] * 3 + [ANY, ANY, VMEM],
        out_specs=(VMEM, SMEM),
        scratch_shapes=[pltpu.SMEM((1,), jnp.int32), pltpu.SemaphoreType.DMA],
        cost_estimate=pl.CostEstimate(flops=0, bytes_accessed=wide_count * count * NT * 4, transcendentals=0),
        name="pack_first",
    )(table, plan, core, own, mate, tiles)


def spill_kernel(base, table, core_ref, own, same, other, plan, fill, started, sem):
    core = core_ref[0]
    started[0] = 0

    @pl.loop(0, fill.shape[0])
    def _(dev):
        fill[dev] = 0

    for half in range(2):

        @pl.loop(0, valid_slots(table, half))
        def _(at):
            dev = owner_of(table[half, at])
            rank = fill[dev]
            fill[dev] = rank + 1
            plan[half, at] = jnp.where(rank < base, dev * 4 + rank, -1)

            @pl.when((rank >= base) & (core == half) & (started[0] < SPILL))
            def _():
                index = started[0]
                started[0] = index + 1
                pltpu.make_async_copy(own.at[at, unit(core)], same.at[index], sem).start()
                pltpu.make_async_copy(own.at[at, unit(1 - core)], other.at[index], sem).start()

    @pl.loop(0, 2 * started[0])
    def _(_):
        pltpu.make_async_copy(own.at[0, unit(0)], same.at[0], sem).wait()


def spill(base, wide_count, table, core, own):
    buffer = jax.ShapeDtypeStruct((SPILL, ROWS, LANES), jnp.bfloat16)
    return pl.pallas_call(
        functools.partial(spill_kernel, base),
        out_shape=(
            buffer,
            buffer,
            jax.ShapeDtypeStruct((2, table.shape[1] - 1), jnp.int32),
            jax.ShapeDtypeStruct((wide_count,), jnp.int32),
        ),
        in_specs=[SMEM, SMEM, ANY],
        out_specs=(VMEM, VMEM, SMEM, SMEM),
        scratch_shapes=[pltpu.SMEM((1,), jnp.int32), pltpu.SemaphoreType.DMA],
        cost_estimate=pl.CostEstimate(flops=0, bytes_accessed=2**20, transcendentals=0),
        name="spill",
    )(table, core, own)


def pack_kernel(base, table, plan, held, core_ref, own, mate, same, other, after, out, fill, theirs, started, taken, sem):
    core = core_ref[0]
    started[0] = 0

    @pl.loop(0, out.shape[0])
    def _(dev):
        fill[dev] = held[dev]
        theirs[dev] = 0

    def place(half, source, guests):
        @pl.loop(0, valid_slots(table, half))
        def _(at):
            code = plan[half, at]

            @pl.when(code >= 0)
            def _():
                started[0] += 1
                rows = source.at[at, unit(core)]
                pltpu.make_async_copy(rows, out.at[code >> 2, unit(code & 3)], sem).start()

        taken[0] = 0

        @pl.loop(0, valid_slots(table, 2 + half))
        def _(at):
            dev = owner_of(table[2 + half, at])
            rank = theirs[dev]
            theirs[dev] = rank + 1

            @pl.when(rank >= base)
            def _():
                index = taken[0]
                slot = fill[dev]
                taken[0] = index + 1

                @pl.when((index < SPILL) & (slot < base))
                def _():
                    fill[dev] = slot + 1
                    started[0] += 1
                    pltpu.make_async_copy(guests.at[index], out.at[dev, unit(slot)], sem).start()

    for half in range(2):

        @pl.when(core == half)
        def _():
            place(half, own, same)

        @pl.when(core != half)
        def _():
            place(half, mate, other)

    @pl.loop(0, started[0])
    def _(_):
        pltpu.make_async_copy(own.at[0, unit(0)], out.at[0, unit(0)], sem).wait()


def pack_planned(base, table, plan, held, core, own, mate, same, other, after):
    wide_count = held.shape[0]
    return pl.pallas_call(
        functools.partial(pack_kernel, base),
        out_shape=jax.ShapeDtypeStruct((wide_count, base * ROWS, LANES), jnp.bfloat16),
        in_specs=[SMEM] * 4 + [ANY] * 5,
        out_specs=VMEM,
        scratch_shapes=[
            pltpu.SMEM((wide_count,), jnp.int32),
            pltpu.SMEM((wide_count,), jnp.int32),
            pltpu.SMEM((1,), jnp.int32),
            pltpu.SMEM((1,), jnp.int32),
            pltpu.SemaphoreType.DMA,
        ],
        cost_estimate=pl.CostEstimate(flops=0, bytes_accessed=wide_count * base * NT * 4, transcendentals=0),
        name="pack_planned",
    )(table, plan, held, core, own, mate, same, other, after)


def table_notes(packed):
    owner = (packed >> LEN_BITS) + 1
    length = jnp.where(packed >= 0, packed & 0xFFFF, 0)
    parts = jnp.concatenate([owner >> 8, owner & 0xFF, length >> 8, length & 0xFF])
    rows = 3 * LANES - parts.shape[0]
    parts = jnp.pad(parts, (0, rows)).reshape(3, LANES)
    return jnp.pad(parts, ((NOTES - 3, 0), (0, 0)))


def read_slots(rows, count):
    notes = rows[::2, count * ROWS : count * ROWS + 3 * count + 1, 0].astype(jnp.float32).astype(jnp.int32)
    fields = notes[:, : 3 * count].reshape(-1, count, 3)
    station, length = fields[..., 0] - 1, fields[..., 1] * 256 + fields[..., 2]
    return station.reshape(-1), length.reshape(-1), notes[:, 3 * count]


def read_table(rows, slots, chips):
    parts = rows[:, -3:, :].astype(jnp.float32).astype(jnp.int32)
    parts = parts.reshape(rows.shape[0], -1)[:, : 4 * slots].reshape(chips, 2, 4, slots)
    return (parts[:, :, 0] * 256 + parts[:, :, 1] - 1).reshape(chips, 2 * slots)


def second_places(owner, column, base):
    chips, entries = owner.shape
    extra = MOST - base
    slots = entries // 2
    listed = owner >= 0
    dev = jnp.where(listed, owner // ST_DEV, -1)
    order = jnp.arange(entries, dtype=jnp.int32)
    earlier = order[None, :] < order[:, None]
    alike = (dev[:, :, None] == dev[:, None, :]) & earlier
    rank = jnp.sum(alike.astype(jnp.int32), axis=2)
    over = listed & (rank >= base)
    near = earlier & (order[None, :] // slots == order[:, None] // slots)
    index = jnp.sum((over[:, None, :] & near).astype(jnp.int32), axis=2)
    sent = over & (index < SPILL)
    guest = jnp.sum((alike & sent[:, None, :]).astype(jnp.int32), axis=2)
    host_dev = jnp.concatenate([dev[chips // 2 :], dev[: chips // 2]])
    host_held = jnp.sum((dev[:, :, None] == host_dev[:, None, :]).astype(jnp.int32), axis=2)
    slot = host_held + guest
    fits = sent & (slot < base)
    chip = jnp.arange(chips, dtype=jnp.int32)[:, None]
    host = (chip + chips // 2) % chips
    code = jnp.where(rank < base, chip * base + rank, chips * base + chip * extra + rank - base)
    code = jnp.where(fits, host * base + slot, code)
    local = column * ST_DEV + jnp.arange(ST_DEV, dtype=jnp.int32)
    chosen = owner[None] == local[:, None, None]
    return jnp.sum(jnp.where(chosen, code[None], 0), axis=(1, 2))


def whiten_kernel(
    part, parts, source, length, picks, got, more, first, twist, second, *refs
):
    token, held, spectra, sem, sems = refs[-5:]
    stops, rows = picks.shape
    white = refs[-6 - parts]
    payload = refs[-5 - parts : -5]
    token[0] = 0
    stations = held.shape[0]
    base = SLOTS[part]
    first_more = got.shape[0] // 2 * base
    batch = 8

    def fetch(rows, code, count, station):
        for seg in range(2):
            source_at = rows.at[2 * (code // count) + seg, unit(code % count)]
            pltpu.make_async_copy(source_at, held.at[station, unit(seg)], sems.at[station // batch]).start()

    @pl.loop(0, stations)
    def _(station):
        code = source[station]

        @pl.when(code < first_more)
        def _():
            fetch(got, code, base, station)

        @pl.when(code >= first_more)
        def _():
            fetch(more, code - first_more, MOST - base, station)

    row = lax.broadcasted_iota(jnp.int32, (2 * ROWS, LANES), 0)
    lane = lax.broadcasted_iota(jnp.int32, (2 * ROWS, LANES), 1)
    left = lax.broadcasted_iota(jnp.int32, (ROWS // 2, LANES), 1) < ROWS
    place = (2 * part + (row & 1)) * NT + (row >> 1) * LANES + lane

    def two_stations(station):
        sides = []
        for at in range(2):
            values = held[station + at].astype(jnp.float32)
            sides.append(jnp.where(place < length[station + at], values, 0.0).astype(jnp.bfloat16))
        values = jnp.concatenate(sides, 1)
        values = jnp.concatenate([values, values], 0)
        mixed = jnp.dot(first[...], values, preferred_element_type=jnp.float32)
        parts = []
        for at in range(2):
            for seg in range(2):
                real = mixed[2 * seg * ROWS : (2 * seg + 1) * ROWS, at * LANES : (at + 1) * LANES]
                imag = mixed[(2 * seg + 1) * ROWS : (2 * seg + 2) * ROWS, at * LANES : (at + 1) * LANES]
                turned_re = real * twist[0] + imag * twist[1]
                turned_im = imag * twist[0] - real * twist[1]
                parts.append(jnp.concatenate([turned_re, turned_im], 1))
        turned = jnp.concatenate(parts, 0)
        high = turned.astype(jnp.bfloat16)
        low = (turned - high.astype(jnp.float32)).astype(jnp.bfloat16)
        upper = jnp.dot(high, second[...], preferred_element_type=jnp.float32)
        lower = jnp.dot(low, second[:, :LANES], preferred_element_type=jnp.float32)
        spectrum = upper[:, :LANES] + (upper[:, LANES:] + lower)
        for at in range(2):
            for seg in range(2):
                begin = (2 * at + seg) * ROWS
                side = spectrum[begin : begin + ROWS]
                power = jnp.sum(side * side, axis=0, keepdims=True)
                power = (power + pltpu.roll(power, LANES // 2, 1)) * (1.0 / ROWS)
                scale = 1.0 / jnp.sqrt(power + 1e-06)
                side = side * scale
                upper, lower = side[: ROWS // 2], side[ROWS // 2 :]
                real = jnp.where(left, upper, pltpu.roll(lower, ROWS, 1))
                imag = jnp.where(left, pltpu.roll(upper, ROWS, 1), lower)
                spectra[station + at, seg, : ROWS // 2] = real.astype(jnp.bfloat16)
                spectra[station + at, seg, ROWS // 2 :] = imag.astype(jnp.bfloat16)

    @pl.loop(0, stations // batch)
    def _(at):
        these = held.at[pl.ds(at * batch, batch)]
        pltpu.make_async_copy(these, these, sems.at[at]).wait()
        for two in range(0, batch, 2):
            two_stations(batch * at + two)

    each = stops // parts
    for piece in range(parts):

        @pl.loop(0, each)
        def _(stop):
            for at in range(rows):
                row = spectra.at[picks[piece * each + stop, at]]
                pltpu.make_async_copy(row, payload[piece].at[stop, at], sem).start()

    whole = pltpu.make_async_copy(spectra, white, sems.at[0])
    whole.start()
    for piece in range(parts):
        pltpu.make_async_copy(payload[piece], payload[piece], sem).wait()
    whole.wait()


def whiten(part, parts, source, length, picks, got, more, tables, after):
    stops, rows = picks.shape
    piece = jax.ShapeDtypeStruct((stops // parts, rows, 2, ROWS, LANES), jnp.bfloat16)
    return pl.pallas_call(
        functools.partial(whiten_kernel, part, parts),
        out_shape=(jax.ShapeDtypeStruct((ST_DEV, 2, ROWS, LANES), jnp.bfloat16),)
        + (piece,) * parts
        + (jax.ShapeDtypeStruct((1,), jnp.int32),),
        in_specs=[SMEM, SMEM, SMEM, ANY, ANY, VMEM, VMEM, VMEM] + [ANY] * len(after),
        out_specs=(ANY,) * (1 + parts) + (SMEM,),
        scratch_shapes=[
            pltpu.VMEM((ST_DEV, 2 * ROWS, LANES), jnp.bfloat16),
            pltpu.VMEM((ST_DEV, 2, ROWS, LANES), jnp.bfloat16),
            pltpu.SemaphoreType.DMA,
            pltpu.SemaphoreType.DMA((ST_DEV // 8,)),
        ],
        cost_estimate=pl.CostEstimate(flops=2**20, bytes_accessed=2**18, transcendentals=0),
        name="whiten",
    )(source, length, picks, got, more, *tables, *after)


def cross_rows(near_pick, near, far, cross, fresh, ready):
    stops, rows = near_pick.shape
    side = rows // 2
    step = 16
    half = ROWS // 2

    @pl.loop(0, stops)
    def _(stop):
        ready(stop)
        for two in range(2):
            first = two * side
            own = [near_pick[stop, first + i] for i in range(side)]

            @pl.loop(0, half // step)
            def _(chunk):
                real = pl.ds(pl.multiple_of(chunk * step, step), step)
                imag = pl.ds(pl.multiple_of(half + chunk * step, step), step)

                def both(ref, row):
                    return [
                        (ref[row, s, real, :].astype(jnp.float32), ref[row, s, imag, :].astype(jnp.float32))
                        for s in range(2)
                    ]

                here = [both(near, own[i]) for i in range(side)]
                for j in range(side):
                    there = both(far.at[stop], first + j)
                    for i in range(side):
                        pair = ((stop * 2 + two) * side + i) * side + j
                        total_re = sum(n[0] * f[0] + n[1] * f[1] for n, f in zip(here[i], there))
                        total_im = sum(n[1] * f[0] - n[0] * f[1] for n, f in zip(here[i], there))
                        for total, add in ((total_re, 0), (total_im, half)):
                            at = pl.ds(pl.multiple_of(pair * ROWS + add + chunk * step, step), step)
                            if fresh:
                                cross[at, :] = total
                            else:
                                cross[at, :] += total


def lag_product(cross, tables, last, out, edge, exact):
    pairs = out.shape[0]
    group = 8
    depth = group * LANES
    half = LAGS // 2
    turns = ROWS // 2 // group

    def product(turn, even):
        base = turn * group
        slabs = [cross[pl.ds(base + k, pairs, stride=ROWS), :] for k in range(group)]
        high = [slab.astype(jnp.bfloat16) for slab in slabs]
        if even:
            total = edge[...]
            for k in range(group):
                total += (slabs[k] if exact else high[k].astype(jnp.float32)) * last[base + k]
            edge[...] = total
        rows = jnp.concatenate(high, 1)
        if exact:
            low = [(slab - part.astype(jnp.float32)).astype(jnp.bfloat16) for slab, part in zip(slabs, high)]
            rows = jnp.concatenate([rows, jnp.concatenate(low, 1)], 0)
        part = jnp.dot(
            rows,
            tables[pl.ds(pl.multiple_of(base * LANES, depth), depth), :],
            preferred_element_type=jnp.float32,
        )
        return part[:pairs] + part[pairs:] if exact else part

    @pl.loop(0, turns)
    def _(turn):
        out[:, :half] += product(turn, True)

    @pl.loop(turns, 2 * turns)
    def _(turn):
        out[:, half:] += product(turn, False)


def first_lag_kernel(stops, near_pick, white, home, *refs):
    far_in = refs[: stops - 1]
    table, last, out, edge, near, far, cross, tables, sem, sems, table_sem = refs[stops - 1 :]
    load = pltpu.make_async_copy(white, near, sem)
    load.start()
    pltpu.make_async_copy(home, far.at[0], sems.at[0]).start()
    for stop in range(1, stops):
        pltpu.make_async_copy(far_in[stop - 1], far.at[stop], sems.at[stop]).start()
    load_table = pltpu.make_async_copy(table, tables, table_sem)
    load_table.start()
    out[...] = jnp.zeros_like(out)
    edge[...] = jnp.zeros_like(edge)
    load.wait()

    def ready(stop):
        pltpu.make_async_copy(far.at[stop], far.at[stop], sems.at[stop]).wait()

    cross_rows(near_pick, near, far, cross, True, ready)
    load_table.wait()
    lag_product(cross, tables, last, out, edge, True)


def last_lag_kernel(
    near_pick, far_at, begun, begun_edge, white, far_in, table, last, mask,
    result, near, far, cross, out, edge, tables, sem, sems, table_sem,
):
    stops = near_pick.shape[0]
    pairs = out.shape[0]
    half = LAGS // 2
    load = pltpu.make_async_copy(white, near, sem.at[0])
    load.start()
    for stop in range(stops):
        pltpu.make_async_copy(far_in.at[far_at[stop]], far.at[stop], sems.at[stop]).start()
    load_table = pltpu.make_async_copy(table, tables, table_sem)
    load_table.start()
    before = [pltpu.make_async_copy(begun, out, sem.at[1]), pltpu.make_async_copy(begun_edge, edge, sem.at[2])]
    for copy in before:
        copy.start()
    load.wait()

    def ready(stop):
        pltpu.make_async_copy(far.at[stop], far.at[stop], sems.at[stop]).wait()

    cross_rows(near_pick, near, far, cross, True, ready)
    load_table.wait()
    for copy in before:
        copy.wait()
    lag_product(cross, tables, last, out, edge, False)
    first_lag = jnp.sum(edge[...], axis=1, keepdims=True)
    lane = lax.broadcasted_iota(jnp.int32, (pairs, LANES), 1)
    mirror = (LANES - lane) % LANES
    first = lane == 0
    listed = mask[...]
    count = half // LANES
    back, ahead = [], []
    for block in range(count):
        even = out[:, block * LANES : (block + 1) * LANES]
        odd = out[:, half + block * LANES : half + (block + 1) * LANES]
        if block == 0:
            first_lag = first_lag + odd
            odd = jnp.where(first, 0.0, odd)
        back.append(even - odd)
        ahead.append(even + odd)
    for block in range(count):
        turned = jnp.take_along_axis(back[count - 1 - block], mirror, axis=1)
        start = first_lag if block == 0 else back[count - block]
        lags = pl.ds(block * LANES, LANES)
        result[:, :, lags] = (jnp.where(first, start, turned) * listed).reshape(result.shape[:2] + (LANES,))
        lags = pl.ds(half + block * LANES, LANES)
        result[:, :, lags] = (ahead[block] * listed).reshape(result.shape[:2] + (LANES,))


def lag_scratch(white, stops, pairs, table):
    return [
        pltpu.VMEM(white.shape, jnp.bfloat16),
        pltpu.VMEM((stops, 8, 2, ROWS, LANES), jnp.bfloat16),
        pltpu.VMEM((pairs * ROWS, LANES), jnp.float32),
    ], [pltpu.VMEM(table.shape, jnp.bfloat16)]


def lagged_first(near_pick, white, home, far, table, last):
    stops, rows = near_pick.shape
    pairs = stops * rows * rows // 2
    scratch, table_scratch = lag_scratch(white, stops, pairs, table)
    return pl.pallas_call(
        functools.partial(first_lag_kernel, stops),
        out_shape=(
            jax.ShapeDtypeStruct((pairs, LAGS), jnp.float32),
            jax.ShapeDtypeStruct((pairs, LANES), jnp.float32),
        ),
        in_specs=[SMEM] + [ANY] * (stops + 2) + [VMEM],
        out_specs=(VMEM, VMEM),
        scratch_shapes=scratch
        + table_scratch
        + [pltpu.SemaphoreType.DMA, pltpu.SemaphoreType.DMA((stops,)), pltpu.SemaphoreType.DMA],
        compiler_params=pltpu.CompilerParams(vmem_limit_bytes=LAG_VMEM),
        cost_estimate=pl.CostEstimate(
            flops=4 * pairs * NF * LAGS, bytes_accessed=16 * 1024 * 1024, transcendentals=0
        ),
        name="lagged_first",
    )(near_pick, white, home, *far, table, last)


def lagged_last(near_pick, far_at, begun, edge, white, far, table, last, mask):
    stops, rows = near_pick.shape
    side = rows // 2
    pairs = mask.shape[0]
    scratch, table_scratch = lag_scratch(white, stops, pairs, table)
    return pl.pallas_call(
        last_lag_kernel,
        out_shape=jax.ShapeDtypeStruct((pairs // side, side, LAGS), jnp.float32),
        in_specs=[SMEM, SMEM] + [ANY] * 5 + [VMEM, VMEM],
        out_specs=VMEM,
        scratch_shapes=scratch
        + [pltpu.VMEM((pairs, LAGS), jnp.float32), pltpu.VMEM((pairs, LANES), jnp.float32)]
        + table_scratch
        + [pltpu.SemaphoreType.DMA((3,)), pltpu.SemaphoreType.DMA((stops,)), pltpu.SemaphoreType.DMA],
        compiler_params=pltpu.CompilerParams(vmem_limit_bytes=LAG_VMEM),
        cost_estimate=pl.CostEstimate(
            flops=2 * pairs * NF * LAGS, bytes_accessed=16 * 1024 * 1024, transcendentals=0
        ),
        name="lagged_last",
    )(near_pick, far_at, begun, edge, white, far, table, last, mask)


def empty(shape):
    return pl.pallas_call(
        lambda out: None,
        out_shape=jax.ShapeDtypeStruct(shape, jnp.bfloat16),
        out_specs=ANY,
        name="empty",
    )()


def on_device(records, lengths, owners, own_pick, visit_pick, pair_mask):
    wide_count = lax.axis_size("wide")
    stops = lax.axis_size("blk")
    column = lax.axis_index("wide")
    group = lax.axis_index("blk")
    core = column % 2
    slots = records.shape[1]
    steps = jnp.arange(stops, dtype=jnp.int32)
    core_at = core.reshape(1)

    def flip(bits):
        return [(i, i ^ bits) for i in range(wide_count)]

    def across(shard, bits):
        return lax.ppermute(shard, "wide", flip(bits))

    over = wide_count // 2
    packed = jnp.where(owners[0] >= 0, (owners[0] << LEN_BITS) + lengths[0], -1)
    counted = jnp.concatenate([packed, jnp.sum((packed >= 0).astype(jnp.int32), keepdims=True)])
    others = [across(counted, bits) for bits in (1, over, over + 1)]
    table = jnp.where(
        core == 0,
        jnp.stack([counted, others[0], others[1], others[2]]),
        jnp.stack([others[0], counted, others[2], others[1]]),
    )

    blocks = records[0].reshape(slots, SEG, ROWS, LANES)

    def halves(part):
        return blocks[:, 2 * part : 2 * part + 2].transpose(0, 2, 1, 3).reshape(slots, 2 * ROWS, LANES)

    def send(payload):
        return lax.all_to_all(payload, "wide", split_axis=0, concat_axis=0, tiled=True)

    own_a = halves(0)
    mate_a = across(own_a, 1)
    base_a, base_b = SLOTS
    plan_a, tiles, _ = plan_rows(base_a, base_b, wide_count, table, table_notes(packed))
    load_a, token = pack_first(base_a, table, plan_a, core_at, own_a, mate_a, tiles)
    got_a = send(load_a)
    own_b = jnp.where(token[0] >= 0, halves(1), 0.0)
    mate_b = across(own_b, 1)
    same_b, other_b, plan, held = spill(base_b, wide_count, table, core_at, own_b)
    same_b, other_b = across(same_b, over), across(other_b, over + 1)
    visits = jnp.where(token[0] >= 0, visit_pick[0, 0].reshape(1, stops, -1), 0)
    bit = 1
    while bit < stops:
        theirs = lax.ppermute(visits, "blk", [(i, i ^ bit) for i in range(stops)])
        upper = (group // bit) % 2 == 1
        visits = jnp.concatenate([jnp.where(upper, theirs, visits), jnp.where(upper, visits, theirs)])
        bit *= 2
    by_dest = visits[steps, (steps - group) % stops]
    by_stop = by_dest[(steps + group) % stops]
    load_b = pack_planned(base_b, table, plan, held, core_at, own_b, mate_b, same_b, other_b, by_stop)
    got_b = send(load_b)

    def late_rows(low, own, mate):
        return send(pack_rows(low, MOST - low, wide_count, table, core_at, own, mate))

    def late():
        first = late_rows(base_a, own_a, mate_a)
        second = late_rows(base_b, own_b, mate_b)
        return (first, second) + read_slots(first, MOST - base_a)[:2]

    def never():
        count = wide_count // 2 * (MOST - base_a)
        rows = [empty((wide_count, (MOST - base) * ROWS + NOTES, LANES)) for base in SLOTS]
        return rows[0], rows[1], jnp.full((count,), -1, jnp.int32), jnp.zeros((count,), jnp.int32)

    station, length, spilled = read_slots(got_a, base_a)
    more_a, more_b, more_station, more_length = lax.cond(jnp.max(spilled) > 0, late, never)
    station = jnp.concatenate([station, more_station])
    length = jnp.concatenate([length, more_length])
    chosen = station[None, :] == jnp.arange(ST_DEV, dtype=jnp.int32)[:, None]
    codes = jnp.arange(station.shape[0], dtype=jnp.int32)
    source_a = jnp.sum(jnp.where(chosen, codes[None], 0), axis=1)
    length = jnp.sum(jnp.where(chosen, length[None], 0), axis=1)

    tables = [jnp.asarray(table) for table in transform_tables()]
    near_pick = own_pick[0, 0].reshape(stops, -1)
    white_a, home, *payload_a, _ = whiten(0, stops, source_a, length, by_stop, got_a, more_a, tables, [])
    far_a = [
        lax.ppermute(payload_a[stop - 1][0], "blk", [(i, (i + stop) % stops) for i in range(stops)])
        for stop in range(1, stops)
    ]
    source_b = second_places(read_table(got_a, slots, wide_count // 2), column, base_b)
    white_b, payload_b, _ = whiten(1, 1, source_b, length, by_dest, got_b, more_b, tables, far_a)
    far_b = lax.all_to_all(payload_b, "blk", split_axis=0, concat_axis=0, tiled=True)

    far_at = (group - steps) % stops
    mask = pair_mask[0, 0].astype(jnp.float32).reshape(-1, 1)
    lags, last = (jnp.asarray(table) for table in lag_tables())
    begun, edge = lagged_first(near_pick, white_a, home[0], far_a, lags, last)
    result = lagged_last(near_pick, far_at, begun, edge, white_b, far_b, lags, last, mask)
    return result.reshape((1, 1) + pair_mask.shape[2:] + (LAGS,))


def solution(mesh):
    return jax.shard_map(
        on_device,
        mesh=mesh,
        in_specs=(
            P("blk", "wide", None, None),
            P("blk", "wide"),
            P("blk", "wide"),
            P("blk", "wide", None, None, None),
            P("blk", "wide", None, None, None),
            P("blk", "wide", None, None, None, None),
        ),
        out_specs=P("blk", "wide", None, None, None, None, None),
        check_vma=False,
    )
```

profile of v0, /device:TPU:1, one launch (start us, length us, event | category | flops | bytes accessed | tf_op | source)
XLA Modules:
  0.0 198.7 jit_solution(1472429657994903736)
XLA Ops:
  0.0 4.5 %slice.78 = bf16[72,2,64,128]{3,1,2,0:T(2,128)(2,1)S(1)} slice(bf16[72,4,64,128]{3,1,2,0:T(4,128)(2,1)} %bitcast.70), slice={[0:72], [0:2], [0:64], [0:128]} | slice | bytes 4718592 | tf_op jit(solution)/shard_map/slice | solution.py:805
  4.5 3.3 %collective-permute-start.3 = (bf16[72,128,128]{2,1,0:T(8,128)(2,1)S(1)}, bf16[72,128,128]{2,1,0:T(8,128)(2,1)}, u32[]{:S(2)}, u32[]{:S(2)}) collective-permute-start(bf16[72,128,128]{2,1,0:T(8,128)(2,1)S(1)} %bitcast.67), channel_id=1, source_target_pairs={{0,8},{8,0},{16,24},{24,16},{32,40},{40,32},{48,56},{56,48},{64,72... | collective-permute-start | bytes 7077896 | tf_op jit(solution)/shard_map/ppermute | solution.py:790
  9.2 1.6 collective-permute-start.1
  12.8 3.5 %plan_rows.1 = (s32[2,72]{1,0:T(2,128)}, bf16[32,16,128]{2,1,0:T(8,128)(2,1)}, s32[32]{0:T(128)}) custom-call(s32[4,73]{1,0:T(4,128)S(1)} %add_select_fusion.1.table, s32[16,128]{1,0:T(8,128)} %pad.9.base), custom_call_target="tpu_custom_call" | custom-call | flops 65536 | bytes 262144 | tf_op jit(solution)/shard_map/plan_rows/pallas_call | solution.py:211
  16.3 4.0 %pack_first.1 = (bf16[32,272,128]{2,1,0:T(8,128)(2,1)}, s32[1]{0:T(128)}) custom-call(s32[4,73]{1,0:T(4,128)S(1)} %add_select_fusion.1.table, s32[2,72]{1,0:T(2,128)} %get-tuple-element.48.plan, s32[1]{0:T(128)} %bitcast.9.core_ref, bf16[72,128,128]{2,1,0:T(8,128)(2,1)S(1)} %bitcast.68, bf16[72,128,128]{2,1,0:T(8,128)(2,1)} %collective-permute-done.3.mate, ...), custom_call_target="tpu_custom_call" | custom-call | bytes 4194304 | tf_op jit(solution)/shard_map/pack_first/pallas_call | solution.py:267
  20.4 8.4 %all-to-all-start.2 = ((bf16[32,272,128]{2,1,0:T(8,128)(2,1)}), bf16[32,272,128]{2,1,0:T(8,128)(2,1)}, u32[]{:S(2)}, u32[]{:S(2)}) async-start(bf16[32,272,128]{2,1,0:T(8,128)(2,1)} %get-tuple-element.50), calls=%async_computation.2 | async-start | bytes 4456448 | tf_op jit(solution)/shard_map/all_to_all | solution.py:808
  29.5 6.0 %broadcast_select_fusion = bf16[72,2,64,128]{3,1,2,0:T(2,128)(2,1)S(1)} fusion(pred[]{:T(512)} %bitcast.14, bf16[72,4,64,128]{3,1,2,0:T(4,128)(2,1)} %bitcast.71), kind=kLoop, calls=%fused_computation.6 | loop fusion | flops 1179648 | bytes 4718593 | tf_op jit(solution)/shard_map/jit(_where)/select_n | solution.py:816
  36.2 2.1 %collective-permute-start.5 = (s32[1,8,8]{2,1,0:T(8,128)S(1)}, s32[1,8,8]{2,1,0:T(8,128)S(1)}, u32[]{:S(2)}, u32[]{:S(2)}) collective-permute-start(s32[1,8,8]{2,1,0:T(8,128)S(1)} %copy.70), channel_id=1, source_target_pairs={{0,1},{1,0},{2,3},{3,2},{4,5},{5,4},{6,7},{7,6},{8,9},{9,8},{10,11... | collective-permute-start | bytes 776 | tf_op jit(solution)/shard_map/ppermute | solution.py:823
  39.7 4.7 %collective-permute-start.6 = (s32[2,8,8]{2,1,0:T(8,128)S(1)}, s32[2,8,8]{2,1,0:T(8,128)S(1)}, u32[]{:S(2)}, u32[]{:S(2)}) collective-permute-start(s32[2,8,8]{2,1,0:T(8,128)S(1)} %pad_add_fusion.3), channel_id=1, source_target_pairs={{0,2},{1,3},{2,0},{3,1},{4,6},{5,7},{6,4},{7,5},{8,10},{9,11},{10,... | collective-permute-start | bytes 1544 | tf_op jit(solution)/shard_map/ppermute | solution.py:823
  45.8 2.0 %collective-permute-start.7 = (s32[4,8,8]{2,1,0:T(8,128)S(1)}, s32[4,8,8]{2,1,0:T(8,128)S(1)}, u32[]{:S(2)}, u32[]{:S(2)}) collective-permute-start(s32[4,8,8]{2,1,0:T(8,128)S(1)} %pad_add_fusion.1), channel_id=1, source_target_pairs={{0,4},{1,5},{2,6},{3,7},{4,0},{5,1},{6,2},{7,3},{8,12},{9,13},{10,... | collective-permute-start | bytes 3080 | tf_op jit(solution)/shard_map/ppermute | solution.py:823
  47.8 2.7 %spill.1 = (bf16[12,64,128]{2,1,0:T(8,128)(2,1)}, bf16[12,64,128]{2,1,0:T(8,128)(2,1)}, s32[2,72]{1,0:T(2,128)}, s32[32]{0:T(128)}) custom-call(s32[4,73]{1,0:T(4,128)S(1)} %add_select_fusion.1.table, s32[1]{0:T(128)} %bitcast.9.core_ref, bf16[72,128,128]{2,1,0:T(8,128)(2,1)S(1)} %bitcast.64), custom_call_target="tpu_custom_call" | custom-call | bytes 1048576 | tf_op jit(solution)/shard_map/spill/pallas_call | solution.py:312
  51.0 3.3 %collective-permute-start.16 = (bf16[12,64,128]{2,1,0:T(8,128)(2,1)}, bf16[12,64,128]{2,1,0:T(8,128)(2,1)S(1)}, u32[]{:S(2)}, u32[]{:S(2)}) collective-permute-start(bf16[12,64,128]{2,1,0:T(8,128)(2,1)} %get-tuple-element.69), channel_id=1, source_target_pairs={{0,136},{8,128},{16,152},{24,144},{32,168},{40,160},{48,184},{56,1... | collective-permute-start | bytes 589832 | tf_op jit(solution)/shard_map/ppermute | solution.py:790
  56.1 2.5 %collective-permute-done.15.same = bf16[12,64,128]{2,1,0:T(8,128)(2,1)S(1)} collective-permute-done((bf16[12,64,128]{2,1,0:T(8,128)(2,1)}, bf16[12,64,128]{2,1,0:T(8,128)(2,1)S(1)}, u32[]{:S(2)}, u32[]{:S(2)}) %collective-permute-start.15) | collective-permute-done | bytes 196640 | tf_op jit(solution)/shard_map/ppermute | solution.py:790
  58.6 10.1 %collective-permute-done.16.other = bf16[12,64,128]{2,1,0:T(8,128)(2,1)S(1)} collective-permute-done((bf16[12,64,128]{2,1,0:T(8,128)(2,1)}, bf16[12,64,128]{2,1,0:T(8,128)(2,1)S(1)}, u32[]{:S(2)}, u32[]{:S(2)}) %collective-permute-start.16) | collective-permute-done | bytes 196640 | tf_op jit(solution)/shard_map/ppermute | solution.py:790
  69.4 4.7 %pack_planned.1 = bf16[32,192,128]{2,1,0:T(8,128)(2,1)} custom-call(s32[4,73]{1,0:T(4,128)S(1)} %add_select_fusion.1.table, s32[2,72]{1,0:T(2,128)} %get-tuple-element.66.plan, s32[32]{0:T(128)} %get-tuple-element.67.held, s32[1]{0:T(128)} %bitcast.9.core_ref, bf16[72,128,128]{2,1,0:T(8,128)(2,1)S(1)} %bitcast.65, ...), custom_call_target="tpu_custom_call" | custom-call | bytes 3145728 | tf_op jit(solution)/shard_map/pack_planned/pallas_call | solution.py:385
  74.1 7.0 %all-to-all-done.2.got = bf16[32,272,128]{2,1,0:T(8,128)(2,1)} async-done(((bf16[32,272,128]{2,1,0:T(8,128)(2,1)}), bf16[32,272,128]{2,1,0:T(8,128)(2,1)}, u32[]{:S(2)}, u32[]{:S(2)}) %all-to-all-start.2) | async-done | bytes 2228256 | tf_op jit(solution)/shard_map/all_to_all | solution.py:808
  83.7 5.5 %all-to-all-start.3 = ((bf16[32,192,128]{2,1,0:T(8,128)(2,1)}), bf16[32,192,128]{2,1,0:T(8,128)(2,1)S(1)}, u32[]{:S(2)}, u32[]{:S(2)}) async-start(bf16[32,192,128]{2,1,0:T(8,128)(2,1)} %pack_planned.1), calls=%async_computation.3 | async-start | bytes 3145728 | tf_op jit(solution)/shard_map/all_to_all | solution.py:808
  90.5 8.1 %whiten.2 = (bf16[24,2,64,128]{3,2,1,0:T(8,128)(2,1)}, bf16[1,8,2,64,128]{4,3,2,1,0:T(8,128)(2,1)}, bf16[1,8,2,64,128]{4,3,2,1,0:T(8,128)(2,1)}, bf16[1,8,2,64,1...) custom-call(s32[24]{0:T(128)} %get-tuple-element.76.source, ...), custom_call_target="tpu_custom_call" | custom-call | flops 1048576 | bytes 262144 | tf_op jit(solution)/shard_map/whiten/pallas_call | solution.py:549
  98.6 2.1 %collective-permute-start.8 = (bf16[8,2,64,128]{3,2,1,0:T(8,128)(2,1)}, bf16[8,2,64,128]{3,2,1,0:T(8,128)(2,1)S(1)}, u32[]{:S(2)}, u32[]{:S(2)}) collective-permute-start(bf16[8,2,64,128]{3,2,1,0:T(8,128)(2,1)} %bitcast.94), channel_id=1, source_target_pairs={{0,1},{1,2},{2,3},{3,4},{4,5},{5,6},{6,7},{7,0},{8,9},{9,10},{10,1... | collective-permute-start | bytes 786440 | tf_op jit(solution)/shard_map/ppermute | solution.py:858
  100.7 4.6 %collective-permute-start.9 = (bf16[8,2,64,128]{3,2,1,0:T(8,128)(2,1)}, bf16[8,2,64,128]{3,2,1,0:T(8,128)(2,1)S(1)}, u32[]{:S(2)}, u32[]{:S(2)}) collective-permute-start(bf16[8,2,64,128]{3,2,1,0:T(8,128)(2,1)} %bitcast.93), channel_id=1, source_target_pairs={{0,2},{1,3},{2,4},{3,5},{4,6},{5,7},{6,0},{7,1},{8,10},{9,11},{10,... | collective-permute-start | bytes 786440 | tf_op jit(solution)/shard_map/ppermute | solution.py:858
  105.3 1.8 collective-permute-start.10
  107.1 2.6 %collective-permute-start.12 = (bf16[8,2,64,128]{3,2,1,0:T(8,128)(2,1)}, bf16[8,2,64,128]{3,2,1,0:T(8,128)(2,1)S(1)}, u32[]{:S(2)}, u32[]{:S(2)}) collective-permute-start(bf16[8,2,64,128]{3,2,1,0:T(8,128)(2,1)} %bitcast.90), channel_id=1, source_target_pairs={{0,5},{1,6},{2,7},{3,0},{4,1},{5,2},{6,3},{7,4},{8,13},{9,14},{10,... | collective-permute-start | bytes 786440 | tf_op jit(solution)/shard_map/ppermute | solution.py:858
  112.7 1.7 convert_reduce_fusion
  114.5 13.3 %collective-permute-done.8.refs_0_ = bf16[8,2,64,128]{3,2,1,0:T(8,128)(2,1)S(1)} collective-permute-done((bf16[8,2,64,128]{3,2,1,0:T(8,128)(2,1)}, bf16[8,2,64,128]{3,2,1,0:T(8,128)(2,1)S(1)}, u32[]{:S(2)}, u32[]{:S(2)}) %collective-permute-start.8) | collective-permute-done | bytes 262176 | tf_op jit(solution)/shard_map/ppermute | solution.py:858
  129.3 1.8 collective-permute-done.10.refs_2_
  131.1 7.9 %collective-permute-done.11.refs_3_ = bf16[8,2,64,128]{3,2,1,0:T(8,128)(2,1)S(1)} collective-permute-done((bf16[8,2,64,128]{3,2,1,0:T(8,128)(2,1)}, bf16[8,2,64,128]{3,2,1,0:T(8,128)(2,1)S(1)}, u32[]{:S(2)}, u32[]{:S(2)}) %collective-permute-start.11) | collective-permute-done | bytes 262176 | tf_op jit(solution)/shard_map/ppermute | solution.py:858
  139.0 3.0 %collective-permute-done.14.refs_6_ = bf16[8,2,64,128]{3,2,1,0:T(8,128)(2,1)S(1)} collective-permute-done((bf16[8,2,64,128]{3,2,1,0:T(8,128)(2,1)}, bf16[8,2,64,128]{3,2,1,0:T(8,128)(2,1)S(1)}, u32[]{:S(2)}, u32[]{:S(2)}) %collective-permute-start.14) | collective-permute-done | bytes 262176 | tf_op jit(solution)/shard_map/ppermute | solution.py:858
  143.2 8.2 %whiten.3 = (bf16[24,2,64,128]{3,2,1,0:T(8,128)(2,1)}, bf16[8,8,2,64,128]{4,3,2,1,0:T(8,128)(2,1)}, s32[1]{0:T(128)}) custom-call(s32[24]{0:T(128)} %select_reduce_fusion.source, s32[24]{0:T(128)} %get-tuple-element.75.length, s32[8,8]{1,0:T(8,128)} %copy-done.3, bf16[32,192,128]{2,1,0:T(8,128)(2,1)} %copy-done.2, ...), custom_call_target="tpu_custom_call" | custom-call | flops 1048576 | bytes 262144 | tf_op jit(solution)/shard_map/whiten/pallas_call | solution.py:549
  151.4 4.2 %all-to-all-start.4 = ((bf16[8,8,2,64,128]{4,3,2,1,0:T(8,128)(2,1)}), bf16[8,8,2,64,128]{4,3,2,1,0:T(8,128)(2,1)S(1)}, u32[]{:S(2)}, u32[]{:S(2)}) async-start(bf16[8,8,2,64,128]{4,3,2,1,0:T(8,128)(2,1)} %get-tuple-element.72), calls=%async_computation.4 | async-start | bytes 4194304 | tf_op jit(solution)/shard_map/all_to_all | solution.py:863
  157.8 14.3 %lagged_first.1 = (f32[256,1024]{1,0:T(8,128)}, f32[256,128]{1,0:T(8,128)}) custom-call(s32[8,8]{1,0:T(8,128)} %copy.77.near_pick, bf16[24,2,64,128]{3,2,1,0:T(8,128)(2,1)} %get-tuple-element.55.white, bf16[8,2,64,128]{3,2,1,0:T(8,128)(2,1)} %bitcast.87, bf16[8,2,64,128]{3,2,1,0:T(8,128)(2,1)} %copy-done.4, bf16[8,2,64,128]{3,2,1,0:T(8,128)(2,1)} %copy-done.5, ...), custom_call_target="tpu_custom_call" | custom-call | flops 4294967296 | bytes 16777216 | tf_op jit(solution)/shard_map/lagged_first/pallas_call | solution.py:726
  172.0 12.1 %all-to-all-done.4.far_in = bf16[8,8,2,64,128]{4,3,2,1,0:T(8,128)(2,1)S(1)} async-done(((bf16[8,8,2,64,128]{4,3,2,1,0:T(8,128)(2,1)}), bf16[8,8,2,64,128]{4,3,2,1,0:T(8,128)(2,1)S(1)}, u32[]{:S(2)}, u32[]{:S(2)}) %all-to-all-start.4) | async-done | bytes 2097184 | tf_op jit(solution)/shard_map/all_to_all | solution.py:863
  185.5 13.0 %lagged_last.1 = f32[64,4,1024]{2,1,0:T(4,128)} custom-call(s32[8,8]{1,0:T(8,128)} %copy.77.near_pick, s32[8]{0:T(128)} %and_select_fusion.4.far_at, f32[256,1024]{1,0:T(8,128)} %get-tuple-element.64.begun, f32[256,128]{1,0:T(8,128)} %get-tuple-element.65.begun_edge, bf16[24,2,64,128]{3,2,1,0:T(8,128)(2,1)} %get-tuple-element.71.white, ...), custom_call_target="tpu_custom_call" | custom-call | flops 2147483648 | bytes 16777216 | tf_op jit(solution)/shard_map/lagged_last/pallas_call | solution.py:750
  (120 shorter events, 22.1 us)
Async XLA Ops:
  0.0 7.8 %copy-start.16 = (s32[1,72]{1,0:T(1,128)S(1)}, s32[1,72]{1,0:T(1,128)}, u32[]{:S(2)}) copy-start(s32[1,72]{1,0:T(1,128)} %param.14) | copy-start | bytes 868
  0.0 7.8 %copy-start.17 = (s32[1,72]{1,0:T(1,128)S(1)}, s32[1,72]{1,0:T(1,128)}, u32[]{:S(2)}) copy-start(s32[1,72]{1,0:T(1,128)} %param.15) | copy-start | bytes 868
  4.5 15.8 %copy-start = (bf16[72,2,64,128]{3,1,2,0:T(2,128)(2,1)}, bf16[72,2,64,128]{3,1,2,0:T(2,128)(2,1)S(1)}, u32[]{:S(2)}) copy-start(bf16[72,2,64,128]{3,1,2,0:T(2,128)(2,1)S(1)} %slice.78) | copy-start | bytes 7077892
  4.5 11.8 %collective-permute-start.3 = (bf16[72,128,128]{2,1,0:T(8,128)(2,1)S(1)}, bf16[72,128,128]{2,1,0:T(8,128)(2,1)}, u32[]{:S(2)}, u32[]{:S(2)}) collective-permute-start(bf16[72,128,128]{2,1,0:T(8,128)(2,1)S(1)} %bitcast.67), channel_id=1, source_target_pairs={{0,8},{8,0},{16,24},{24,16},{32,40},{40,32},{48,56},{56,48},{64,72... | collective-permute-start | bytes 7077896 | tf_op jit(solution)/shard_map/ppermute | solution.py:790
  9.2 3.6 %collective-permute-start.2 = (s32[73]{0:T(128)S(1)}, s32[73]{0:T(128)S(1)}, u32[]{:S(2)}, u32[]{:S(2)}) collective-permute-start(s32[73]{0:T(128)S(1)} %pad_add_fusion.5), channel_id=1, source_target_pairs={{0,136},{8,128},{16,152},{24,144},{32,168},{40,160},{48,184},{56,1... | collective-permute-start | bytes 884 | tf_op jit(solution)/shard_map/ppermute | solution.py:790
  9.2 3.5 %collective-permute-start.1 = (s32[73]{0:T(128)S(1)}, s32[73]{0:T(128)S(1)}, u32[]{:S(2)}, u32[]{:S(2)}) collective-permute-start(s32[73]{0:T(128)S(1)} %pad_add_fusion.5), channel_id=1, source_target_pairs={{0,128},{8,136},{16,144},{24,152},{32,160},{40,168},{48,176},{56,1... | collective-permute-start | bytes 884 | tf_op jit(solution)/shard_map/ppermute | solution.py:790
  10.8 2.0 collective-permute-start
  20.4 60.7 %all-to-all-start.2 = ((bf16[32,272,128]{2,1,0:T(8,128)(2,1)}), bf16[32,272,128]{2,1,0:T(8,128)(2,1)}, u32[]{:S(2)}, u32[]{:S(2)}) async-start(bf16[32,272,128]{2,1,0:T(8,128)(2,1)} %get-tuple-element.50), calls=%async_computation.2 | async-start | bytes 4456448 | tf_op jit(solution)/shard_map/all_to_all | solution.py:808
  29.5 6.6 %copy-start.14 = (s32[1,1,8,2,4]{2,4,3,1,0:T(4,128)S(1)}, s32[1,1,8,2,4]{2,4,3,1,0:T(4,128)}, u32[]{:S(2)}) copy-start(s32[1,1,8,2,4]{2,4,3,1,0:T(4,128)} %param.17) | copy-start | bytes 772
  35.5 20.7 %collective-permute-start.4 = (bf16[72,128,128]{2,1,0:T(8,128)(2,1)S(1)}, bf16[72,128,128]{2,1,0:T(8,128)(2,1)}, u32[]{:S(2)}, u32[]{:S(2)}) collective-permute-start(bf16[72,128,128]{2,1,0:T(8,128)(2,1)S(1)} %bitcast.63), channel_id=1, source_target_pairs={{0,8},{8,0},{16,24},{24,16},{32,40},{40,32},{48,56},{56,48},{64,72... | collective-permute-start | bytes 7077896 | tf_op jit(solution)/shard_map/ppermute | solution.py:790
  36.2 3.5 %collective-permute-start.5 = (s32[1,8,8]{2,1,0:T(8,128)S(1)}, s32[1,8,8]{2,1,0:T(8,128)S(1)}, u32[]{:S(2)}, u32[]{:S(2)}) collective-permute-start(s32[1,8,8]{2,1,0:T(8,128)S(1)} %copy.70), channel_id=1, source_target_pairs={{0,1},{1,0},{2,3},{3,2},{4,5},{5,4},{6,7},{7,6},{8,9},{9,8},{10,11... | collective-permute-start | bytes 776 | tf_op jit(solution)/shard_map/ppermute | solution.py:823
  39.7 6.1 %collective-permute-start.6 = (s32[2,8,8]{2,1,0:T(8,128)S(1)}, s32[2,8,8]{2,1,0:T(8,128)S(1)}, u32[]{:S(2)}, u32[]{:S(2)}) collective-permute-start(s32[2,8,8]{2,1,0:T(8,128)S(1)} %pad_add_fusion.3), channel_id=1, source_target_pairs={{0,2},{1,3},{2,0},{3,1},{4,6},{5,7},{6,4},{7,5},{8,10},{9,11},{10,... | collective-permute-start | bytes 1544 | tf_op jit(solution)/shard_map/ppermute | solution.py:823
  45.8 8.6 %collective-permute-start.7 = (s32[4,8,8]{2,1,0:T(8,128)S(1)}, s32[4,8,8]{2,1,0:T(8,128)S(1)}, u32[]{:S(2)}, u32[]{:S(2)}) collective-permute-start(s32[4,8,8]{2,1,0:T(8,128)S(1)} %pad_add_fusion.1), channel_id=1, source_target_pairs={{0,4},{1,5},{2,6},{3,7},{4,0},{5,1},{6,2},{7,3},{8,12},{9,13},{10,... | collective-permute-start | bytes 3080 | tf_op jit(solution)/shard_map/ppermute | solution.py:823
  50.5 8.1 %collective-permute-start.15 = (bf16[12,64,128]{2,1,0:T(8,128)(2,1)}, bf16[12,64,128]{2,1,0:T(8,128)(2,1)S(1)}, u32[]{:S(2)}, u32[]{:S(2)}) collective-permute-start(bf16[12,64,128]{2,1,0:T(8,128)(2,1)} %get-tuple-element.68), channel_id=1, source_target_pairs={{0,128},{8,136},{16,144},{24,152},{32,160},{40,168},{48,176},{56,1... | collective-permute-start | bytes 589832 | tf_op jit(solution)/shard_map/ppermute | solution.py:790
  51.0 17.7 %collective-permute-start.16 = (bf16[12,64,128]{2,1,0:T(8,128)(2,1)}, bf16[12,64,128]{2,1,0:T(8,128)(2,1)S(1)}, u32[]{:S(2)}, u32[]{:S(2)}) collective-permute-start(bf16[12,64,128]{2,1,0:T(8,128)(2,1)} %get-tuple-element.69), channel_id=1, source_target_pairs={{0,136},{8,128},{16,152},{24,144},{32,168},{40,160},{48,184},{56,1... | collective-permute-start | bytes 589832 | tf_op jit(solution)/shard_map/ppermute | solution.py:790
  55.0 19.1 %copy-start.3 = (s32[8,8]{1,0:T(8,128)}, s32[8,8]{1,0:T(8,128)S(1)}, u32[]{:S(2)}) copy-start(s32[8,8]{1,0:T(8,128)S(1)} %gather_fusion) | copy-start | bytes 772
  58.6 10.2 %copy-start.11 = (bf16[12,64,128]{2,1,0:T(8,128)(2,1)}, bf16[12,64,128]{2,1,0:T(8,128)(2,1)S(1)}, u32[]{:S(2)}) copy-start(bf16[12,64,128]{2,1,0:T(8,128)(2,1)S(1)} %collective-permute-done.15.same) | copy-start | bytes 589828
  83.7 58.3 %all-to-all-start.3 = ((bf16[32,192,128]{2,1,0:T(8,128)(2,1)}), bf16[32,192,128]{2,1,0:T(8,128)(2,1)S(1)}, u32[]{:S(2)}, u32[]{:S(2)}) async-start(bf16[32,192,128]{2,1,0:T(8,128)(2,1)} %pack_planned.1), calls=%async_computation.3 | async-start | bytes 3145728 | tf_op jit(solution)/shard_map/all_to_all | solution.py:808
  98.6 29.2 %collective-permute-start.8 = (bf16[8,2,64,128]{3,2,1,0:T(8,128)(2,1)}, bf16[8,2,64,128]{3,2,1,0:T(8,128)(2,1)S(1)}, u32[]{:S(2)}, u32[]{:S(2)}) collective-permute-start(bf16[8,2,64,128]{3,2,1,0:T(8,128)(2,1)} %bitcast.94), channel_id=1, source_target_pairs={{0,1},{1,2},{2,3},{3,4},{4,5},{5,6},{6,7},{7,0},{8,9},{9,10},{10,1... | collective-permute-start | bytes 786440 | tf_op jit(solution)/shard_map/ppermute | solution.py:858
  100.7 27.0 %collective-permute-start.9 = (bf16[8,2,64,128]{3,2,1,0:T(8,128)(2,1)}, bf16[8,2,64,128]{3,2,1,0:T(8,128)(2,1)S(1)}, u32[]{:S(2)}, u32[]{:S(2)}) collective-permute-start(bf16[8,2,64,128]{3,2,1,0:T(8,128)(2,1)} %bitcast.93), channel_id=1, source_target_pairs={{0,2},{1,3},{2,4},{3,5},{4,6},{5,7},{6,0},{7,1},{8,10},{9,11},{10,... | collective-permute-start | bytes 786440 | tf_op jit(solution)/shard_map/ppermute | solution.py:858
  105.3 25.8 %collective-permute-start.10 = (bf16[8,2,64,128]{3,2,1,0:T(8,128)(2,1)}, bf16[8,2,64,128]{3,2,1,0:T(8,128)(2,1)S(1)}, u32[]{:S(2)}, u32[]{:S(2)}) collective-permute-start(bf16[8,2,64,128]{3,2,1,0:T(8,128)(2,1)} %bitcast.92), channel_id=1, source_target_pairs={{0,3},{1,4},{2,5},{3,6},{4,7},{5,0},{6,1},{7,2},{8,11},{9,12},{10,... | collective-permute-start | bytes 786440 | tf_op jit(solution)/shard_map/ppermute | solution.py:858
  107.1 31.9 %collective-permute-start.11 = (bf16[8,2,64,128]{3,2,1,0:T(8,128)(2,1)}, bf16[8,2,64,128]{3,2,1,0:T(8,128)(2,1)S(1)}, u32[]{:S(2)}, u32[]{:S(2)}) collective-permute-start(bf16[8,2,64,128]{3,2,1,0:T(8,128)(2,1)} %bitcast.91), channel_id=1, source_target_pairs={{0,4},{1,5},{2,6},{3,7},{4,0},{5,1},{6,2},{7,3},{8,12},{9,13},{10,... | collective-permute-start | bytes 786440 | tf_op jit(solution)/shard_map/ppermute | solution.py:858
  107.1 31.9 %collective-permute-start.12 = (bf16[8,2,64,128]{3,2,1,0:T(8,128)(2,1)}, bf16[8,2,64,128]{3,2,1,0:T(8,128)(2,1)S(1)}, u32[]{:S(2)}, u32[]{:S(2)}) collective-permute-start(bf16[8,2,64,128]{3,2,1,0:T(8,128)(2,1)} %bitcast.90), channel_id=1, source_target_pairs={{0,5},{1,6},{2,7},{3,0},{4,1},{5,2},{6,3},{7,4},{8,13},{9,14},{10,... | collective-permute-start | bytes 786440 | tf_op jit(solution)/shard_map/ppermute | solution.py:858
  127.8 14.3 %copy-start.4 = (bf16[8,2,64,128]{3,2,1,0:T(8,128)(2,1)}, bf16[8,2,64,128]{3,2,1,0:T(8,128)(2,1)S(1)}, u32[]{:S(2)}) copy-start(bf16[8,2,64,128]{3,2,1,0:T(8,128)(2,1)S(1)} %collective-permute-done.8.refs_0_) | copy-start | bytes 786436
  127.8 11.2 %collective-permute-start.13 = (bf16[8,2,64,128]{3,2,1,0:T(8,128)(2,1)}, bf16[8,2,64,128]{3,2,1,0:T(8,128)(2,1)S(1)}, u32[]{:S(2)}, u32[]{:S(2)}) collective-permute-start(bf16[8,2,64,128]{3,2,1,0:T(8,128)(2,1)} %bitcast.89), channel_id=1, source_target_pairs={{0,6},{1,7},{2,0},{3,1},{4,2},{5,3},{6,4},{7,5},{8,14},{9,15},{10,... | collective-permute-start | bytes 786440 | tf_op jit(solution)/shard_map/ppermute | solution.py:858
  127.8 14.3 %copy-start.5 = (bf16[8,2,64,128]{3,2,1,0:T(8,128)(2,1)}, bf16[8,2,64,128]{3,2,1,0:T(8,128)(2,1)S(1)}, u32[]{:S(2)}) copy-start(bf16[8,2,64,128]{3,2,1,0:T(8,128)(2,1)S(1)} %collective-permute-done.9.refs_1_) | copy-start | bytes 786436
  127.8 14.2 %collective-permute-start.14 = (bf16[8,2,64,128]{3,2,1,0:T(8,128)(2,1)}, bf16[8,2,64,128]{3,2,1,0:T(8,128)(2,1)S(1)}, u32[]{:S(2)}, u32[]{:S(2)}) collective-permute-start(bf16[8,2,64,128]{3,2,1,0:T(8,128)(2,1)} %bitcast.88), channel_id=1, source_target_pairs={{0,7},{1,0},{2,1},{3,2},{4,3},{5,4},{6,5},{7,6},{8,15},{9,8},{10,9... | collective-permute-start | bytes 786440 | tf_op jit(solution)/shard_map/ppermute | solution.py:858
  131.1 10.9 %copy-start.6 = (bf16[8,2,64,128]{3,2,1,0:T(8,128)(2,1)}, bf16[8,2,64,128]{3,2,1,0:T(8,128)(2,1)S(1)}, u32[]{:S(2)}) copy-start(bf16[8,2,64,128]{3,2,1,0:T(8,128)(2,1)S(1)} %collective-permute-done.10.refs_2_) | copy-start | bytes 786436
  139.0 3.1 %copy-start.9 = (bf16[8,2,64,128]{3,2,1,0:T(8,128)(2,1)}, bf16[8,2,64,128]{3,2,1,0:T(8,128)(2,1)S(1)}, u32[]{:S(2)}) copy-start(bf16[8,2,64,128]{3,2,1,0:T(8,128)(2,1)S(1)} %collective-permute-done.13.refs_5_) | copy-start | bytes 786436
  151.4 4.2 %copy-start.15 = (s32[1,1,8,2,4]{2,4,3,1,0:T(4,128)S(1)}, s32[1,1,8,2,4]{2,4,3,1,0:T(4,128)}, u32[]{:S(2)}) copy-start(s32[1,1,8,2,4]{2,4,3,1,0:T(4,128)} %param.16) | copy-start | bytes 772
  151.4 4.9 %copy-start.13 = (s32[1,1,8,2,4,4]{2,5,4,3,1,0:T(4,128)S(1)}, s32[1,1,8,2,4,4]{2,5,4,3,1,0:T(4,128)}, u32[]{:S(2)}) copy-start(s32[1,1,8,2,4,4]{2,5,4,3,1,0:T(4,128)} %param.18) | copy-start | bytes 3076
  151.4 32.7 %all-to-all-start.4 = ((bf16[8,8,2,64,128]{4,3,2,1,0:T(8,128)(2,1)}), bf16[8,8,2,64,128]{4,3,2,1,0:T(8,128)(2,1)S(1)}, u32[]{:S(2)}, u32[]{:S(2)}) async-start(bf16[8,8,2,64,128]{4,3,2,1,0:T(8,128)(2,1)} %get-tuple-element.72), calls=%async_computation.4 | async-start | bytes 4194304 | tf_op jit(solution)/shard_map/all_to_all | solution.py:863
  (6 other events, 10.1 us)
where the time goes:
time: 201 us; the launch traced here: 199 us
  waiting for transfers between devices  60.6 us (30%)
  Pallas kernels  58.3 us (29%)
  starting transfers between devices  48.1 us (24%)
  other arithmetic  17.3 us (9%)
  local copies, waits for them, and re-layouts  12.3 us (6%)
    ppermute x7, waiting for transfers between devices, on_device(): lax.ppermute(payload_a[stop - 1][0], 'blk', [(i, (i + stop) % stops) for...  26 us
    pallas_call x2, Pallas kernels, whiten(): pl.pallas_call(functools.partial(whiten_kernel, part, parts), out_shape=(...  16.3 us
    pallas_call x1, Pallas kernels, lagged_first(): pl.pallas_call(functools.partial(first_lag_kernel, stops), out_shape=(jax...  14.3 us
    all_to_all x2, starting transfers between devices, send(): lax.all_to_all(payload, 'wide', split_axis=0, concat_axis=0, tiled=True)  13.9 us
    pallas_call x1, Pallas kernels, lagged_last(): pl.pallas_call(last_lag_kernel, out_shape=jax.ShapeDtypeStruct((pairs //...  13 us
    ppermute x7, waiting for transfers between devices, across(): return lax.ppermute(shard, 'wide', flip(bits))  12.7 us
    all_to_all x1, waiting for transfers between devices, on_device(): lax.all_to_all(payload_b, 'blk', split_axis=0, concat_axis=0, tiled=True)  12.1 us
    ppermute x7, starting transfers between devices, on_device(): lax.ppermute(payload_a[stop - 1][0], 'blk', [(i, (i + stop) % stops) for...  11.5 us
  transfers between devices with their start and end apart: 20, of which 10 were waited for; matrix products, arithmetic and copies ran while one was open for 10% of the time, Pallas kernels for 17%

commit v1 on v0

--- a/solution.py
+++ b/solution.py
@@ -605,7 +605,7 @@
 
 def lag_product(cross, tables, last, out, edge, exact):
     pairs = out.shape[0]
-    group = 8
+    group = 8 if exact else 16
     depth = group * LANES
     half = LAGS // 2
     turns = ROWS // 2 // group

time: 201 us -> 201 us (level)
  starting transfers between devices: 48.1 us -> 50.7 us
    all_to_all x1, starting transfers between devices: 4.2 us -> 6.6 us  [on_device(): lax.all_to_all(payload_b, 'blk', split_axis=0, concat_axis=0, tiled=True)]
    ppermute x7, waiting for transfers between devices: 26 us -> 23.7 us  [on_device(): lax.ppermute(payload_a[stop - 1][0], 'blk', [(i, (i + stop) % stops) for...]
where the time goes in v1:
time: 201 us; the launch traced here: 199 us
  waiting for transfers between devices  60 us (30%)
  Pallas kernels  57.1 us (28%)
  starting transfers between devices  50.7 us (25%)
  other arithmetic  17.3 us (9%)
  local copies, waits for them, and re-layouts  12.3 us (6%)
    ppermute x7, waiting for transfers between devices, on_device(): lax.ppermute(payload_a[stop - 1][0], 'blk', [(i, (i + stop) % stops) for...  23.7 us
    pallas_call x2, Pallas kernels, whiten(): pl.pallas_call(functools.partial(whiten_kernel, part, parts), out_shape=(...  16.3 us
    all_to_all x2, starting transfers between devices, send(): lax.all_to_all(payload, 'wide', split_axis=0, concat_axis=0, tiled=True)  14.6 us
    pallas_call x1, Pallas kernels, lagged_first(): pl.pallas_call(functools.partial(first_lag_kernel, stops), out_shape=(jax...  14.3 us
    ppermute x7, waiting for transfers between devices, across(): return lax.ppermute(shard, 'wide', flip(bits))  12.8 us
    ppermute x7, starting transfers between devices, on_device(): lax.ppermute(payload_a[stop - 1][0], 'blk', [(i, (i + stop) % stops) for...  12.4 us
    pallas_call x1, Pallas kernels, lagged_last(): pl.pallas_call(last_lag_kernel, out_shape=jax.ShapeDtypeStruct((pairs //...  12.4 us
    all_to_all x1, waiting for transfers between devices, on_device(): lax.all_to_all(payload_b, 'blk', split_axis=0, concat_axis=0, tiled=True)  12.1 us
  transfers between devices with their start and end apart: 20, of which 10 were waited for; matrix products, arithmetic and copies ran while one was open for 10% of the time, Pallas kernels for 17%

profile of v1, /device:TPU:1, one launch (start us, length us, event | category | flops | bytes accessed | tf_op | source)
XLA Modules:
  0.0 199.4 jit_solution(5742111913212187423)
XLA Ops:
  0.0 4.5 %slice.78 = bf16[72,2,64,128]{3,1,2,0:T(2,128)(2,1)S(1)} slice(bf16[72,4,64,128]{3,1,2,0:T(4,128)(2,1)} %bitcast.70), slice={[0:72], [0:2], [0:64], [0:128]} | slice | bytes 4718592 | tf_op jit(solution)/shard_map/slice | solution.py:805
  4.5 3.3 %collective-permute-start.3 = (bf16[72,128,128]{2,1,0:T(8,128)(2,1)S(1)}, bf16[72,128,128]{2,1,0:T(8,128)(2,1)}, u32[]{:S(2)}, u32[]{:S(2)}) collective-permute-start(bf16[72,128,128]{2,1,0:T(8,128)(2,1)S(1)} %bitcast.67), channel_id=1, source_target_pairs={{0,8},{8,0},{16,24},{24,16},{32,40},{40,32},{48,56},{56,48},{64,72... | collective-permute-start | bytes 7077896 | tf_op jit(solution)/shard_map/ppermute | solution.py:790
  9.2 1.6 collective-permute-start.1
  12.8 3.6 %plan_rows.1 = (s32[2,72]{1,0:T(2,128)}, bf16[32,16,128]{2,1,0:T(8,128)(2,1)}, s32[32]{0:T(128)}) custom-call(s32[4,73]{1,0:T(4,128)S(1)} %add_select_fusion.1.table, s32[16,128]{1,0:T(8,128)} %pad.9.base), custom_call_target="tpu_custom_call" | custom-call | flops 65536 | bytes 262144 | tf_op jit(solution)/shard_map/plan_rows/pallas_call | solution.py:211
  16.5 3.5 %pack_first.1 = (bf16[32,272,128]{2,1,0:T(8,128)(2,1)}, s32[1]{0:T(128)}) custom-call(s32[4,73]{1,0:T(4,128)S(1)} %add_select_fusion.1.table, s32[2,72]{1,0:T(2,128)} %get-tuple-element.48.plan, s32[1]{0:T(128)} %bitcast.9.core_ref, bf16[72,128,128]{2,1,0:T(8,128)(2,1)S(1)} %bitcast.68, bf16[72,128,128]{2,1,0:T(8,128)(2,1)} %collective-permute-done.3.mate, ...), custom_call_target="tpu_custom_call" | custom-call | bytes 4194304 | tf_op jit(solution)/shard_map/pack_first/pallas_call | solution.py:267
  20.0 9.0 %all-to-all-start.2 = ((bf16[32,272,128]{2,1,0:T(8,128)(2,1)}), bf16[32,272,128]{2,1,0:T(8,128)(2,1)}, u32[]{:S(2)}, u32[]{:S(2)}) async-start(bf16[32,272,128]{2,1,0:T(8,128)(2,1)} %get-tuple-element.50), calls=%async_computation.2 | async-start | bytes 4456448 | tf_op jit(solution)/shard_map/all_to_all | solution.py:808
  29.7 6.0 %broadcast_select_fusion = bf16[72,2,64,128]{3,1,2,0:T(2,128)(2,1)S(1)} fusion(pred[]{:T(512)} %bitcast.14, bf16[72,4,64,128]{3,1,2,0:T(4,128)(2,1)} %bitcast.71), kind=kLoop, calls=%fused_computation.6 | loop fusion | flops 1179648 | bytes 4718593 | tf_op jit(solution)/shard_map/jit(_where)/select_n | solution.py:816
  36.4 3.6 %collective-permute-start.5 = (s32[1,8,8]{2,1,0:T(8,128)S(1)}, s32[1,8,8]{2,1,0:T(8,128)S(1)}, u32[]{:S(2)}, u32[]{:S(2)}) collective-permute-start(s32[1,8,8]{2,1,0:T(8,128)S(1)} %copy.70), channel_id=1, source_target_pairs={{0,1},{1,0},{2,3},{3,2},{4,5},{5,4},{6,7},{7,6},{8,9},{9,8},{10,11... | collective-permute-start | bytes 776 | tf_op jit(solution)/shard_map/ppermute | solution.py:823
  41.4 1.5 collective-permute-start.6
  42.9 3.0 %collective-permute-done.6 = s32[2,8,8]{2,1,0:T(8,128)S(1)} collective-permute-done((s32[2,8,8]{2,1,0:T(8,128)S(1)}, s32[2,8,8]{2,1,0:T(8,128)S(1)}, u32[]{:S(2)}, u32[]{:S(2)}) %collective-permute-start.6) | collective-permute-done | bytes 544 | tf_op jit(solution)/shard_map/ppermute | solution.py:823
  45.9 2.6 %collective-permute-start.7 = (s32[4,8,8]{2,1,0:T(8,128)S(1)}, s32[4,8,8]{2,1,0:T(8,128)S(1)}, u32[]{:S(2)}, u32[]{:S(2)}) collective-permute-start(s32[4,8,8]{2,1,0:T(8,128)S(1)} %pad_add_fusion.1), channel_id=1, source_target_pairs={{0,4},{1,5},{2,6},{3,7},{4,0},{5,1},{6,2},{7,3},{8,12},{9,13},{10,... | collective-permute-start | bytes 3080 | tf_op jit(solution)/shard_map/ppermute | solution.py:823
  48.5 2.6 %spill.1 = (bf16[12,64,128]{2,1,0:T(8,128)(2,1)}, bf16[12,64,128]{2,1,0:T(8,128)(2,1)}, s32[2,72]{1,0:T(2,128)}, s32[32]{0:T(128)}) custom-call(s32[4,73]{1,0:T(4,128)S(1)} %add_select_fusion.1.table, s32[1]{0:T(128)} %bitcast.9.core_ref, bf16[72,128,128]{2,1,0:T(8,128)(2,1)S(1)} %bitcast.64), custom_call_target="tpu_custom_call" | custom-call | bytes 1048576 | tf_op jit(solution)/shard_map/spill/pallas_call | solution.py:312
  52.4 2.3 %collective-permute-start.16 = (bf16[12,64,128]{2,1,0:T(8,128)(2,1)}, bf16[12,64,128]{2,1,0:T(8,128)(2,1)S(1)}, u32[]{:S(2)}, u32[]{:S(2)}) collective-permute-start(bf16[12,64,128]{2,1,0:T(8,128)(2,1)} %get-tuple-element.69), channel_id=1, source_target_pairs={{0,136},{8,128},{16,152},{24,144},{32,168},{40,160},{48,184},{56,1... | collective-permute-start | bytes 589832 | tf_op jit(solution)/shard_map/ppermute | solution.py:790
  56.4 2.8 %collective-permute-done.15.same = bf16[12,64,128]{2,1,0:T(8,128)(2,1)S(1)} collective-permute-done((bf16[12,64,128]{2,1,0:T(8,128)(2,1)}, bf16[12,64,128]{2,1,0:T(8,128)(2,1)S(1)}, u32[]{:S(2)}, u32[]{:S(2)}) %collective-permute-start.15) | collective-permute-done | bytes 196640 | tf_op jit(solution)/shard_map/ppermute | solution.py:790
  59.2 10.0 %collective-permute-done.16.other = bf16[12,64,128]{2,1,0:T(8,128)(2,1)S(1)} collective-permute-done((bf16[12,64,128]{2,1,0:T(8,128)(2,1)}, bf16[12,64,128]{2,1,0:T(8,128)(2,1)S(1)}, u32[]{:S(2)}, u32[]{:S(2)}) %collective-permute-start.16) | collective-permute-done | bytes 196640 | tf_op jit(solution)/shard_map/ppermute | solution.py:790
  69.9 4.5 %pack_planned.1 = bf16[32,192,128]{2,1,0:T(8,128)(2,1)} custom-call(s32[4,73]{1,0:T(4,128)S(1)} %add_select_fusion.1.table, s32[2,72]{1,0:T(2,128)} %get-tuple-element.66.plan, s32[32]{0:T(128)} %get-tuple-element.67.held, s32[1]{0:T(128)} %bitcast.9.core_ref, bf16[72,128,128]{2,1,0:T(8,128)(2,1)S(1)} %bitcast.65, ...), custom_call_target="tpu_custom_call" | custom-call | bytes 3145728 | tf_op jit(solution)/shard_map/pack_planned/pallas_call | solution.py:385
  74.4 7.0 %all-to-all-done.2.got = bf16[32,272,128]{2,1,0:T(8,128)(2,1)} async-done(((bf16[32,272,128]{2,1,0:T(8,128)(2,1)}), bf16[32,272,128]{2,1,0:T(8,128)(2,1)}, u32[]{:S(2)}, u32[]{:S(2)}) %all-to-all-start.2) | async-done | bytes 2228256 | tf_op jit(solution)/shard_map/all_to_all | solution.py:808
  84.0 5.5 %all-to-all-start.3 = ((bf16[32,192,128]{2,1,0:T(8,128)(2,1)}), bf16[32,192,128]{2,1,0:T(8,128)(2,1)S(1)}, u32[]{:S(2)}, u32[]{:S(2)}) async-start(bf16[32,192,128]{2,1,0:T(8,128)(2,1)} %pack_planned.1), calls=%async_computation.3 | async-start | bytes 3145728 | tf_op jit(solution)/shard_map/all_to_all | solution.py:808
  90.7 8.1 %whiten.2 = (bf16[24,2,64,128]{3,2,1,0:T(8,128)(2,1)}, bf16[1,8,2,64,128]{4,3,2,1,0:T(8,128)(2,1)}, bf16[1,8,2,64,128]{4,3,2,1,0:T(8,128)(2,1)}, bf16[1,8,2,64,1...) custom-call(s32[24]{0:T(128)} %get-tuple-element.76.source, ...), custom_call_target="tpu_custom_call" | custom-call | flops 1048576 | bytes 262144 | tf_op jit(solution)/shard_map/whiten/pallas_call | solution.py:549
  98.8 3.6 %collective-permute-start.8 = (bf16[8,2,64,128]{3,2,1,0:T(8,128)(2,1)}, bf16[8,2,64,128]{3,2,1,0:T(8,128)(2,1)S(1)}, u32[]{:S(2)}, u32[]{:S(2)}) collective-permute-start(bf16[8,2,64,128]{3,2,1,0:T(8,128)(2,1)} %bitcast.94), channel_id=1, source_target_pairs={{0,1},{1,2},{2,3},{3,4},{4,5},{5,6},{6,7},{7,0},{8,9},{9,10},{10,1... | collective-permute-start | bytes 786440 | tf_op jit(solution)/shard_map/ppermute | solution.py:858
  103.5 4.8 %collective-permute-start.10 = (bf16[8,2,64,128]{3,2,1,0:T(8,128)(2,1)}, bf16[8,2,64,128]{3,2,1,0:T(8,128)(2,1)S(1)}, u32[]{:S(2)}, u32[]{:S(2)}) collective-permute-start(bf16[8,2,64,128]{3,2,1,0:T(8,128)(2,1)} %bitcast.92), channel_id=1, source_target_pairs={{0,3},{1,4},{2,5},{3,6},{4,7},{5,0},{6,1},{7,2},{8,11},{9,12},{10,... | collective-permute-start | bytes 786440 | tf_op jit(solution)/shard_map/ppermute | solution.py:858
  108.3 2.7 %collective-permute-start.12 = (bf16[8,2,64,128]{3,2,1,0:T(8,128)(2,1)}, bf16[8,2,64,128]{3,2,1,0:T(8,128)(2,1)S(1)}, u32[]{:S(2)}, u32[]{:S(2)}) collective-permute-start(bf16[8,2,64,128]{3,2,1,0:T(8,128)(2,1)} %bitcast.90), channel_id=1, source_target_pairs={{0,5},{1,6},{2,7},{3,0},{4,1},{5,2},{6,3},{7,4},{8,13},{9,14},{10,... | collective-permute-start | bytes 786440 | tf_op jit(solution)/shard_map/ppermute | solution.py:858
  113.9 1.7 convert_reduce_fusion
  115.7 13.6 %collective-permute-done.8.refs_0_ = bf16[8,2,64,128]{3,2,1,0:T(8,128)(2,1)S(1)} collective-permute-done((bf16[8,2,64,128]{3,2,1,0:T(8,128)(2,1)}, bf16[8,2,64,128]{3,2,1,0:T(8,128)(2,1)S(1)}, u32[]{:S(2)}, u32[]{:S(2)}) %collective-permute-start.8) | collective-permute-done | bytes 262176 | tf_op jit(solution)/shard_map/ppermute | solution.py:858
  130.7 1.6 collective-permute-done.10.refs_2_
  132.4 7.1 %collective-permute-done.11.refs_3_ = bf16[8,2,64,128]{3,2,1,0:T(8,128)(2,1)S(1)} collective-permute-done((bf16[8,2,64,128]{3,2,1,0:T(8,128)(2,1)}, bf16[8,2,64,128]{3,2,1,0:T(8,128)(2,1)S(1)}, u32[]{:S(2)}, u32[]{:S(2)}) %collective-permute-start.11) | collective-permute-done | bytes 262176 | tf_op jit(solution)/shard_map/ppermute | solution.py:858
  139.5 1.4 collective-permute-done.14.refs_6_
  142.1 8.2 %whiten.3 = (bf16[24,2,64,128]{3,2,1,0:T(8,128)(2,1)}, bf16[8,8,2,64,128]{4,3,2,1,0:T(8,128)(2,1)}, s32[1]{0:T(128)}) custom-call(s32[24]{0:T(128)} %select_reduce_fusion.source, s32[24]{0:T(128)} %get-tuple-element.75.length, s32[8,8]{1,0:T(8,128)} %copy-done.3, bf16[32,192,128]{2,1,0:T(8,128)(2,1)} %copy-done.2, ...), custom_call_target="tpu_custom_call" | custom-call | flops 1048576 | bytes 262144 | tf_op jit(solution)/shard_map/whiten/pallas_call | solution.py:549
  150.3 6.6 %all-to-all-start.4 = ((bf16[8,8,2,64,128]{4,3,2,1,0:T(8,128)(2,1)}), bf16[8,8,2,64,128]{4,3,2,1,0:T(8,128)(2,1)S(1)}, u32[]{:S(2)}, u32[]{:S(2)}) async-start(bf16[8,8,2,64,128]{4,3,2,1,0:T(8,128)(2,1)} %get-tuple-element.72), calls=%async_computation.4 | async-start | bytes 4194304 | tf_op jit(solution)/shard_map/all_to_all | solution.py:863
  159.1 14.3 %lagged_first.1 = (f32[256,1024]{1,0:T(8,128)}, f32[256,128]{1,0:T(8,128)}) custom-call(s32[8,8]{1,0:T(8,128)} %copy.77.near_pick, bf16[24,2,64,128]{3,2,1,0:T(8,128)(2,1)} %get-tuple-element.55.white, bf16[8,2,64,128]{3,2,1,0:T(8,128)(2,1)} %bitcast.87, bf16[8,2,64,128]{3,2,1,0:T(8,128)(2,1)} %copy-done.4, bf16[8,2,64,128]{3,2,1,0:T(8,128)(2,1)} %copy-done.5, ...), custom_call_target="tpu_custom_call" | custom-call | flops 4294967296 | bytes 16777216 | tf_op jit(solution)/shard_map/lagged_first/pallas_call | solution.py:726
  173.4 12.1 %all-to-all-done.4.far_in = bf16[8,8,2,64,128]{4,3,2,1,0:T(8,128)(2,1)S(1)} async-done(((bf16[8,8,2,64,128]{4,3,2,1,0:T(8,128)(2,1)}), bf16[8,8,2,64,128]{4,3,2,1,0:T(8,128)(2,1)S(1)}, u32[]{:S(2)}, u32[]{:S(2)}) %all-to-all-start.4) | async-done | bytes 2097184 | tf_op jit(solution)/shard_map/all_to_all | solution.py:863
  186.8 12.4 %lagged_last.1 = f32[64,4,1024]{2,1,0:T(4,128)} custom-call(s32[8,8]{1,0:T(8,128)} %copy.77.near_pick, s32[8]{0:T(128)} %and_select_fusion.4.far_at, f32[256,1024]{1,0:T(8,128)} %get-tuple-element.64.begun, f32[256,128]{1,0:T(8,128)} %get-tuple-element.65.begun_edge, bf16[24,2,64,128]{3,2,1,0:T(8,128)(2,1)} %get-tuple-element.71.white, ...), custom_call_target="tpu_custom_call" | custom-call | flops 2147483648 | bytes 16777216 | tf_op jit(solution)/shard_map/lagged_last/pallas_call | solution.py:750
  (120 shorter events, 22.5 us)
Async XLA Ops:
  0.0 7.8 %copy-start.16 = (s32[1,72]{1,0:T(1,128)S(1)}, s32[1,72]{1,0:T(1,128)}, u32[]{:S(2)}) copy-start(s32[1,72]{1,0:T(1,128)} %param.14) | copy-start | bytes 868
  0.0 7.8 %copy-start.17 = (s32[1,72]{1,0:T(1,128)S(1)}, s32[1,72]{1,0:T(1,128)}, u32[]{:S(2)}) copy-start(s32[1,72]{1,0:T(1,128)} %param.15) | copy-start | bytes 868
  4.5 15.5 %copy-start = (bf16[72,2,64,128]{3,1,2,0:T(2,128)(2,1)}, bf16[72,2,64,128]{3,1,2,0:T(2,128)(2,1)S(1)}, u32[]{:S(2)}) copy-start(bf16[72,2,64,128]{3,1,2,0:T(2,128)(2,1)S(1)} %slice.78) | copy-start | bytes 7077892
  4.5 11.9 %collective-permute-start.3 = (bf16[72,128,128]{2,1,0:T(8,128)(2,1)S(1)}, bf16[72,128,128]{2,1,0:T(8,128)(2,1)}, u32[]{:S(2)}, u32[]{:S(2)}) collective-permute-start(bf16[72,128,128]{2,1,0:T(8,128)(2,1)S(1)} %bitcast.67), channel_id=1, source_target_pairs={{0,8},{8,0},{16,24},{24,16},{32,40},{40,32},{48,56},{56,48},{64,72... | collective-permute-start | bytes 7077896 | tf_op jit(solution)/shard_map/ppermute | solution.py:790
  9.2 3.6 %collective-permute-start.2 = (s32[73]{0:T(128)S(1)}, s32[73]{0:T(128)S(1)}, u32[]{:S(2)}, u32[]{:S(2)}) collective-permute-start(s32[73]{0:T(128)S(1)} %pad_add_fusion.5), channel_id=1, source_target_pairs={{0,136},{8,128},{16,152},{24,144},{32,168},{40,160},{48,184},{56,1... | collective-permute-start | bytes 884 | tf_op jit(solution)/shard_map/ppermute | solution.py:790
  9.2 3.5 %collective-permute-start.1 = (s32[73]{0:T(128)S(1)}, s32[73]{0:T(128)S(1)}, u32[]{:S(2)}, u32[]{:S(2)}) collective-permute-start(s32[73]{0:T(128)S(1)} %pad_add_fusion.5), channel_id=1, source_target_pairs={{0,128},{8,136},{16,144},{24,152},{32,160},{40,168},{48,176},{56,1... | collective-permute-start | bytes 884 | tf_op jit(solution)/shard_map/ppermute | solution.py:790
  10.8 2.0 collective-permute-start
  20.0 61.3 %all-to-all-start.2 = ((bf16[32,272,128]{2,1,0:T(8,128)(2,1)}), bf16[32,272,128]{2,1,0:T(8,128)(2,1)}, u32[]{:S(2)}, u32[]{:S(2)}) async-start(bf16[32,272,128]{2,1,0:T(8,128)(2,1)} %get-tuple-element.50), calls=%async_computation.2 | async-start | bytes 4456448 | tf_op jit(solution)/shard_map/all_to_all | solution.py:808
  29.7 6.6 %copy-start.14 = (s32[1,1,8,2,4]{2,4,3,1,0:T(4,128)S(1)}, s32[1,1,8,2,4]{2,4,3,1,0:T(4,128)}, u32[]{:S(2)}) copy-start(s32[1,1,8,2,4]{2,4,3,1,0:T(4,128)} %param.17) | copy-start | bytes 772
  35.7 20.7 %collective-permute-start.4 = (bf16[72,128,128]{2,1,0:T(8,128)(2,1)S(1)}, bf16[72,128,128]{2,1,0:T(8,128)(2,1)}, u32[]{:S(2)}, u32[]{:S(2)}) collective-permute-start(bf16[72,128,128]{2,1,0:T(8,128)(2,1)S(1)} %bitcast.63), channel_id=1, source_target_pairs={{0,8},{8,0},{16,24},{24,16},{32,40},{40,32},{48,56},{56,48},{64,72... | collective-permute-start | bytes 7077896 | tf_op jit(solution)/shard_map/ppermute | solution.py:790
  36.4 5.0 %collective-permute-start.5 = (s32[1,8,8]{2,1,0:T(8,128)S(1)}, s32[1,8,8]{2,1,0:T(8,128)S(1)}, u32[]{:S(2)}, u32[]{:S(2)}) collective-permute-start(s32[1,8,8]{2,1,0:T(8,128)S(1)} %copy.70), channel_id=1, source_target_pairs={{0,1},{1,0},{2,3},{3,2},{4,5},{5,4},{6,7},{7,6},{8,9},{9,8},{10,11... | collective-permute-start | bytes 776 | tf_op jit(solution)/shard_map/ppermute | solution.py:823
  41.4 4.5 %collective-permute-start.6 = (s32[2,8,8]{2,1,0:T(8,128)S(1)}, s32[2,8,8]{2,1,0:T(8,128)S(1)}, u32[]{:S(2)}, u32[]{:S(2)}) collective-permute-start(s32[2,8,8]{2,1,0:T(8,128)S(1)} %pad_add_fusion.3), channel_id=1, source_target_pairs={{0,2},{1,3},{2,0},{3,1},{4,6},{5,7},{6,4},{7,5},{8,10},{9,11},{10,... | collective-permute-start | bytes 1544 | tf_op jit(solution)/shard_map/ppermute | solution.py:823
  45.9 8.8 %collective-permute-start.7 = (s32[4,8,8]{2,1,0:T(8,128)S(1)}, s32[4,8,8]{2,1,0:T(8,128)S(1)}, u32[]{:S(2)}, u32[]{:S(2)}) collective-permute-start(s32[4,8,8]{2,1,0:T(8,128)S(1)} %pad_add_fusion.1), channel_id=1, source_target_pairs={{0,4},{1,5},{2,6},{3,7},{4,0},{5,1},{6,2},{7,3},{8,12},{9,13},{10,... | collective-permute-start | bytes 3080 | tf_op jit(solution)/shard_map/ppermute | solution.py:823
  51.1 8.1 %collective-permute-start.15 = (bf16[12,64,128]{2,1,0:T(8,128)(2,1)}, bf16[12,64,128]{2,1,0:T(8,128)(2,1)S(1)}, u32[]{:S(2)}, u32[]{:S(2)}) collective-permute-start(bf16[12,64,128]{2,1,0:T(8,128)(2,1)} %get-tuple-element.68), channel_id=1, source_target_pairs={{0,128},{8,136},{16,144},{24,152},{32,160},{40,168},{48,176},{56,1... | collective-permute-start | bytes 589832 | tf_op jit(solution)/shard_map/ppermute | solution.py:790
  52.4 16.8 %collective-permute-start.16 = (bf16[12,64,128]{2,1,0:T(8,128)(2,1)}, bf16[12,64,128]{2,1,0:T(8,128)(2,1)S(1)}, u32[]{:S(2)}, u32[]{:S(2)}) collective-permute-start(bf16[12,64,128]{2,1,0:T(8,128)(2,1)} %get-tuple-element.69), channel_id=1, source_target_pairs={{0,136},{8,128},{16,152},{24,144},{32,168},{40,160},{48,184},{56,1... | collective-permute-start | bytes 589832 | tf_op jit(solution)/shard_map/ppermute | solution.py:790
  55.3 19.1 %copy-start.3 = (s32[8,8]{1,0:T(8,128)}, s32[8,8]{1,0:T(8,128)S(1)}, u32[]{:S(2)}) copy-start(s32[8,8]{1,0:T(8,128)S(1)} %gather_fusion) | copy-start | bytes 772
  59.2 10.0 %copy-start.11 = (bf16[12,64,128]{2,1,0:T(8,128)(2,1)}, bf16[12,64,128]{2,1,0:T(8,128)(2,1)S(1)}, u32[]{:S(2)}) copy-start(bf16[12,64,128]{2,1,0:T(8,128)(2,1)S(1)} %collective-permute-done.15.same) | copy-start | bytes 589828
  84.0 57.0 %all-to-all-start.3 = ((bf16[32,192,128]{2,1,0:T(8,128)(2,1)}), bf16[32,192,128]{2,1,0:T(8,128)(2,1)S(1)}, u32[]{:S(2)}, u32[]{:S(2)}) async-start(bf16[32,192,128]{2,1,0:T(8,128)(2,1)} %pack_planned.1), calls=%async_computation.3 | async-start | bytes 3145728 | tf_op jit(solution)/shard_map/all_to_all | solution.py:808
  98.8 30.4 %collective-permute-start.8 = (bf16[8,2,64,128]{3,2,1,0:T(8,128)(2,1)}, bf16[8,2,64,128]{3,2,1,0:T(8,128)(2,1)S(1)}, u32[]{:S(2)}, u32[]{:S(2)}) collective-permute-start(bf16[8,2,64,128]{3,2,1,0:T(8,128)(2,1)} %bitcast.94), channel_id=1, source_target_pairs={{0,1},{1,2},{2,3},{3,4},{4,5},{5,6},{6,7},{7,0},{8,9},{9,10},{10,1... | collective-permute-start | bytes 786440 | tf_op jit(solution)/shard_map/ppermute | solution.py:858
  102.5 26.8 %collective-permute-start.9 = (bf16[8,2,64,128]{3,2,1,0:T(8,128)(2,1)}, bf16[8,2,64,128]{3,2,1,0:T(8,128)(2,1)S(1)}, u32[]{:S(2)}, u32[]{:S(2)}) collective-permute-start(bf16[8,2,64,128]{3,2,1,0:T(8,128)(2,1)} %bitcast.93), channel_id=1, source_target_pairs={{0,2},{1,3},{2,4},{3,5},{4,6},{5,7},{6,0},{7,1},{8,10},{9,11},{10,... | collective-permute-start | bytes 786440 | tf_op jit(solution)/shard_map/ppermute | solution.py:858
  103.5 28.9 %collective-permute-start.10 = (bf16[8,2,64,128]{3,2,1,0:T(8,128)(2,1)}, bf16[8,2,64,128]{3,2,1,0:T(8,128)(2,1)S(1)}, u32[]{:S(2)}, u32[]{:S(2)}) collective-permute-start(bf16[8,2,64,128]{3,2,1,0:T(8,128)(2,1)} %bitcast.92), channel_id=1, source_target_pairs={{0,3},{1,4},{2,5},{3,6},{4,7},{5,0},{6,1},{7,2},{8,11},{9,12},{10,... | collective-permute-start | bytes 786440 | tf_op jit(solution)/shard_map/ppermute | solution.py:858
  108.3 31.2 %collective-permute-start.11 = (bf16[8,2,64,128]{3,2,1,0:T(8,128)(2,1)}, bf16[8,2,64,128]{3,2,1,0:T(8,128)(2,1)S(1)}, u32[]{:S(2)}, u32[]{:S(2)}) collective-permute-start(bf16[8,2,64,128]{3,2,1,0:T(8,128)(2,1)} %bitcast.91), channel_id=1, source_target_pairs={{0,4},{1,5},{2,6},{3,7},{4,0},{5,1},{6,2},{7,3},{8,12},{9,13},{10,... | collective-permute-start | bytes 786440 | tf_op jit(solution)/shard_map/ppermute | solution.py:858
  108.3 31.2 %collective-permute-start.12 = (bf16[8,2,64,128]{3,2,1,0:T(8,128)(2,1)}, bf16[8,2,64,128]{3,2,1,0:T(8,128)(2,1)S(1)}, u32[]{:S(2)}, u32[]{:S(2)}) collective-permute-start(bf16[8,2,64,128]{3,2,1,0:T(8,128)(2,1)} %bitcast.90), channel_id=1, source_target_pairs={{0,5},{1,6},{2,7},{3,0},{4,1},{5,2},{6,3},{7,4},{8,13},{9,14},{10,... | collective-permute-start | bytes 786440 | tf_op jit(solution)/shard_map/ppermute | solution.py:858
  129.2 11.7 %copy-start.4 = (bf16[8,2,64,128]{3,2,1,0:T(8,128)(2,1)}, bf16[8,2,64,128]{3,2,1,0:T(8,128)(2,1)S(1)}, u32[]{:S(2)}) copy-start(bf16[8,2,64,128]{3,2,1,0:T(8,128)(2,1)S(1)} %collective-permute-done.8.refs_0_) | copy-start | bytes 786436
  129.2 10.3 %collective-permute-start.13 = (bf16[8,2,64,128]{3,2,1,0:T(8,128)(2,1)}, bf16[8,2,64,128]{3,2,1,0:T(8,128)(2,1)S(1)}, u32[]{:S(2)}, u32[]{:S(2)}) collective-permute-start(bf16[8,2,64,128]{3,2,1,0:T(8,128)(2,1)} %bitcast.89), channel_id=1, source_target_pairs={{0,6},{1,7},{2,0},{3,1},{4,2},{5,3},{6,4},{7,5},{8,14},{9,15},{10,... | collective-permute-start | bytes 786440 | tf_op jit(solution)/shard_map/ppermute | solution.py:858
  129.2 11.7 %copy-start.5 = (bf16[8,2,64,128]{3,2,1,0:T(8,128)(2,1)}, bf16[8,2,64,128]{3,2,1,0:T(8,128)(2,1)S(1)}, u32[]{:S(2)}) copy-start(bf16[8,2,64,128]{3,2,1,0:T(8,128)(2,1)S(1)} %collective-permute-done.9.refs_1_) | copy-start | bytes 786436
  129.2 11.7 %collective-permute-start.14 = (bf16[8,2,64,128]{3,2,1,0:T(8,128)(2,1)}, bf16[8,2,64,128]{3,2,1,0:T(8,128)(2,1)S(1)}, u32[]{:S(2)}, u32[]{:S(2)}) collective-permute-start(bf16[8,2,64,128]{3,2,1,0:T(8,128)(2,1)} %bitcast.88), channel_id=1, source_target_pairs={{0,7},{1,0},{2,1},{3,2},{4,3},{5,4},{6,5},{7,6},{8,15},{9,8},{10,9... | collective-permute-start | bytes 786440 | tf_op jit(solution)/shard_map/ppermute | solution.py:858
  132.4 8.6 %copy-start.6 = (bf16[8,2,64,128]{3,2,1,0:T(8,128)(2,1)}, bf16[8,2,64,128]{3,2,1,0:T(8,128)(2,1)S(1)}, u32[]{:S(2)}) copy-start(bf16[8,2,64,128]{3,2,1,0:T(8,128)(2,1)S(1)} %collective-permute-done.10.refs_2_) | copy-start | bytes 786436
  139.5 1.5 copy-start.9
  150.3 6.6 %copy-start.15 = (s32[1,1,8,2,4]{2,4,3,1,0:T(4,128)S(1)}, s32[1,1,8,2,4]{2,4,3,1,0:T(4,128)}, u32[]{:S(2)}) copy-start(s32[1,1,8,2,4]{2,4,3,1,0:T(4,128)} %param.16) | copy-start | bytes 772
  150.3 7.3 %copy-start.13 = (s32[1,1,8,2,4,4]{2,5,4,3,1,0:T(4,128)S(1)}, s32[1,1,8,2,4,4]{2,5,4,3,1,0:T(4,128)}, u32[]{:S(2)}) copy-start(s32[1,1,8,2,4,4]{2,5,4,3,1,0:T(4,128)} %param.18) | copy-start | bytes 3076
  150.3 35.2 %all-to-all-start.4 = ((bf16[8,8,2,64,128]{4,3,2,1,0:T(8,128)(2,1)}), bf16[8,8,2,64,128]{4,3,2,1,0:T(8,128)(2,1)S(1)}, u32[]{:S(2)}, u32[]{:S(2)}) async-start(bf16[8,8,2,64,128]{4,3,2,1,0:T(8,128)(2,1)} %get-tuple-element.72), calls=%async_computation.4 | async-start | bytes 4194304 | tf_op jit(solution)/shard_map/all_to_all | solution.py:863
  (6 other events, 6.9 us)
